TPU v7x, 32 devices: a whole 2x2x4 slice. The times are simulated.
32 devices in a mesh: replica: 2 (over y), shard: 16 (over z, x, core).
Axes of the slice: x: 2, y: 2, z: 4, core: 2. Of those that a mesh axis runs over, the one named last changes fastest.
Arguments:
- tokens: bfloat16 [4096, 1024], P(('replica', 'shard')), may hold values from -6 to 6
- norm_gain: bfloat16 [1024], P('shard'), may hold values from 0.5 to 1.5
- w_inner: bfloat16 [1024, 2048], P(None, 'shard'), may hold values from -0.1875 to 0.1875
- w_gate: bfloat16 [1024, 2048], P(None, 'shard'), may hold values from -0.1875 to 0.1875
- conv_weight: bfloat16 [4, 2048], P(None, 'shard'), may hold values from -3 to 3
- conv_bias: bfloat16 [2048], P('shard'), may hold values from -3 to 3
- w_proj: bfloat16 [2048, 96], P('shard'), may hold values from -0.125 to 0.125
- w_step: bfloat16 [64, 2048], P(None, 'shard'), may hold values from -0.75 to 0.75
- step_bias: bfloat16 [2048], P('shard'), may hold values from -6.5 to -2.296875
- a_log: bfloat16 [16, 2048], P(None, 'shard'), may hold values from 0 to 2.765625
- skip_gain: bfloat16 [2048], P('shard'), may hold values from 0.5 to 1.5
- w_out: bfloat16 [2048, 1024], P('shard'), may hold values from -0.125 to 0.125
- cotangent: bfloat16 [4096, 1024], P(('replica', 'shard')), may hold values from -6 to 6
- lengths: int32 [32], P(('replica', 'shard')), may hold values from 32 to 128, as said below
Outputs:
- output: bfloat16 [4096, 1024], P(('replica', 'shard'))
- grad_tokens: float32 [4096, 1024], P(('replica', 'shard'))
- grad_norm_gain: float32 [1024], P('shard')
- grad_w_inner: float32 [1024, 2048], P(None, 'shard')
- grad_w_gate: float32 [1024, 2048], P(None, 'shard')
- grad_conv_weight: float32 [4, 2048], P(None, 'shard')
- grad_conv_bias: float32 [2048], P('shard')
- grad_w_proj: float32 [2048, 96], P('shard')
- grad_w_step: float32 [64, 2048], P(None, 'shard')
- grad_step_bias: float32 [2048], P('shard')
- grad_a_log: float32 [16, 2048], P(None, 'shard')
- grad_skip_gain: float32 [2048], P('shard')
- grad_w_out: float32 [2048, 1024], P('shard')
Inputs may be any that keep to these rules, and one draw needn't show every extreme that they name: lengths[i] is the number of valid positions at the start of slot i, the rest of the slot being padding; some slot has exactly 128 and some other exactly 32.
All inputs are finite; a program needn't handle non-finite values.
Results may differ from a plain program's by a relative error of at most 0.02.
Values may be sent and summed in bfloat16 or wider, within the bound.
A program may use at most 192 MiB of HBM per device.

v0:
```python
from functools import partial

import jax
import jax.numpy as jnp
from jax import lax
from jax.sharding import PartitionSpec as P

RANK = 64
STATE = 16
CONV = 4
BLOCK = 64


EPS = 1e-05
HIGH = lax.Precision.HIGHEST


def combine(earlier, later):
    return (earlier[0] * later[0], later[0] * earlier[1] + later[1])


def silu_slope(pre_act):
    logistic = jax.nn.sigmoid(pre_act)
    return logistic * (1.0 + pre_act * (1.0 - logistic))


def block_states(start_state, step_size, in_map, conv_out, decay_rates):
    decays = jnp.exp(step_size[:, None, :] * decay_rates[None, :, :])
    driven = step_size[:, None, :] * in_map[:, :, None] * conv_out[:, None, :]
    driven = driven.at[0].add(decays[0] * start_state)
    states = lax.associative_scan(combine, (decays, driven), axis=0)[1]
    return (decays, states)


def scan_forward(start_state, pieces, decay_rates):
    step_size, in_map, out_map, conv_out = pieces
    decays, states = block_states(start_state, step_size, in_map, conv_out, decay_rates)
    mixed_out = jnp.einsum("tn,tne->te", out_map, states, precision=HIGH)
    return (states[-1], (start_state, mixed_out))


def scan_backward(carried, pieces, decay_rates):
    adjoint_next, grad_rates = carried
    step_size, in_map, out_map, conv_out, d_mixed, start_state = pieces
    decays, states = block_states(start_state, step_size, in_map, conv_out, decay_rates)
    d_states = out_map[:, :, None] * d_mixed[:, None, :]
    d_states = d_states.at[-1].add(adjoint_next)
    shifted = jnp.concatenate([decays[1:], jnp.zeros_like(decays[:1])], axis=0)
    adjoint = lax.associative_scan(combine, (shifted[::-1], d_states[::-1]), axis=0)[1][::-1]
    previous = jnp.concatenate([start_state[None], states[:-1]], axis=0)
    d_decays = adjoint * previous * decays
    weighted = adjoint * step_size[:, None, :]
    d_step = jnp.sum(
        d_decays * decay_rates[None] + adjoint * in_map[:, :, None] * conv_out[:, None, :], axis=1
    )
    grad_rates = grad_rates + jnp.sum(d_decays * step_size[:, None, :], axis=0)
    d_in_map = jnp.sum(weighted * conv_out[:, None, :], axis=2)
    d_out_map = jnp.sum(d_mixed[:, None, :] * states, axis=2)
    d_conv = jnp.sum(weighted * in_map[:, :, None], axis=1)
    return ((decays[0] * adjoint[0], grad_rates), (d_step, d_in_map, d_out_map, d_conv))


def local(
    tokens,
    norm_gain,
    w_inner,
    w_gate,
    conv_weight,
    conv_bias,
    w_proj,
    w_step,
    step_bias,
    a_log,
    skip_gain,
    w_out,
    cotangent,
    lengths,
):
    gathered = (
        lax.all_gather(norm_gain, "shard", axis=0, tiled=True),
        lax.all_gather(w_inner, "shard", axis=1, tiled=True),
        lax.all_gather(w_gate, "shard", axis=1, tiled=True),
        lax.all_gather(conv_weight, "shard", axis=1, tiled=True),
        lax.all_gather(conv_bias, "shard", axis=0, tiled=True),
        lax.all_gather(w_proj, "shard", axis=0, tiled=True),
        lax.all_gather(w_step, "shard", axis=1, tiled=True),
        lax.all_gather(step_bias, "shard", axis=0, tiled=True),
        lax.all_gather(a_log, "shard", axis=1, tiled=True),
        lax.all_gather(skip_gain, "shard", axis=0, tiled=True),
        lax.all_gather(w_out, "shard", axis=0, tiled=True),
    )
    (
        gain_full,
        inner_full,
        gate_full,
        conv_full,
        conv_shift,
        proj_full,
        step_full,
        step_shift,
        rates_log,
        skip_full,
        out_full,
    ) = gathered
    row_count = tokens.shape[0]
    blocks = row_count // BLOCK

    def to_blocks(tensor):
        return tensor.reshape(blocks, BLOCK, tensor.shape[1])

    residual = tokens.astype(jnp.float32)
    valid_mask = (jnp.arange(row_count, dtype=jnp.int32) < lengths[0]).astype(jnp.float32)[:, None]
    inv_rms = lax.rsqrt(jnp.mean(residual * residual, axis=1, keepdims=True) + EPS)
    normed = (residual * inv_rms * gain_full.astype(jnp.float32)).astype(jnp.bfloat16)
    inner_pre = jnp.dot(normed, inner_full, preferred_element_type=jnp.float32)
    gate_pre = jnp.dot(normed, gate_full, preferred_element_type=jnp.float32)
    conv_taps = conv_full.astype(jnp.float32)
    padded = jnp.pad(inner_pre, ((CONV - 1, 0), (0, 0)))
    conv_pre = jnp.broadcast_to(conv_shift.astype(jnp.float32), inner_pre.shape)
    for offset in range(CONV):
        conv_pre = conv_pre + conv_taps[offset] * padded[offset : offset + row_count]
    conv_out = jax.nn.silu(conv_pre)
    conv_low = conv_out.astype(jnp.bfloat16)
    projected = jnp.dot(conv_low, proj_full, preferred_element_type=jnp.float32)
    step_low = projected[:, :RANK].astype(jnp.bfloat16)
    in_map = projected[:, RANK : RANK + STATE]
    out_map = projected[:, RANK + STATE :]
    step_pre = jnp.dot(step_low, step_full, preferred_element_type=jnp.float32) + step_shift.astype(
        jnp.float32
    )
    step_size = jax.nn.softplus(step_pre)
    decay_rates = -jnp.exp(rates_log.astype(jnp.float32))
    inner_width = conv_out.shape[1]
    zero_state = jnp.zeros((STATE, inner_width), jnp.float32)
    _, (starts, scanned) = lax.scan(
        partial(scan_forward, decay_rates=decay_rates),
        zero_state,
        (to_blocks(step_size), to_blocks(in_map), to_blocks(out_map), to_blocks(conv_out)),
    )
    skip_vals = skip_full.astype(jnp.float32)
    mixed_out = scanned.reshape(row_count, inner_width) + skip_vals * conv_out
    gate_act = jax.nn.silu(gate_pre)
    gated_out = (mixed_out * gate_act).astype(jnp.bfloat16)
    branch = jnp.dot(gated_out, out_full, preferred_element_type=jnp.float32)
    output = (residual + valid_mask * branch).astype(jnp.bfloat16)
    back_weights = (
        lax.all_gather(norm_gain, "shard", axis=0, tiled=True),
        lax.all_gather(w_inner, "shard", axis=1, tiled=True),
        lax.all_gather(w_gate, "shard", axis=1, tiled=True),
        lax.all_gather(conv_weight, "shard", axis=1, tiled=True),
        lax.all_gather(conv_bias, "shard", axis=0, tiled=True),
        lax.all_gather(w_proj, "shard", axis=0, tiled=True),
        lax.all_gather(w_step, "shard", axis=1, tiled=True),
        lax.all_gather(step_bias, "shard", axis=0, tiled=True),
        lax.all_gather(a_log, "shard", axis=1, tiled=True),
        lax.all_gather(skip_gain, "shard", axis=0, tiled=True),
        lax.all_gather(w_out, "shard", axis=0, tiled=True),
    )
    gain_back = back_weights[0].astype(jnp.float32)
    inner_back = back_weights[1]
    gate_back = back_weights[2]
    taps_back = back_weights[3].astype(jnp.float32)
    proj_back = back_weights[5]
    step_back = back_weights[6]
    out_back = back_weights[10]
    d_out = cotangent.astype(jnp.float32)
    d_branch = (d_out * valid_mask).astype(jnp.bfloat16)
    grad_out = jnp.einsum("te,td->ed", gated_out, d_branch, preferred_element_type=jnp.float32)
    d_gated = jnp.einsum("td,ed->te", d_branch, out_back, preferred_element_type=jnp.float32)
    d_mixed = d_gated * gate_act
    d_gate = (d_gated * mixed_out * silu_slope(gate_pre)).astype(jnp.bfloat16)
    grad_skip = jnp.sum(d_mixed * conv_out, axis=0)
    (_, grad_rates), (d_step, d_in_map, d_out_map, d_conv_scan) = lax.scan(
        partial(scan_backward, decay_rates=decay_rates),
        (zero_state, zero_state),
        (
            to_blocks(step_size),
            to_blocks(in_map),
            to_blocks(out_map),
            to_blocks(conv_out),
            to_blocks(d_mixed),
            starts,
        ),
        reverse=True,
    )
    grad_log = grad_rates * decay_rates
    d_conv = d_mixed * skip_vals + d_conv_scan.reshape(row_count, inner_width)
    d_step_pre = d_step.reshape(row_count, inner_width) * jax.nn.sigmoid(step_pre)
    grad_step_shift = jnp.sum(d_step_pre, axis=0)
    d_step_low = d_step_pre.astype(jnp.bfloat16)
    grad_step = jnp.einsum("tr,te->re", step_low, d_step_low, preferred_element_type=jnp.float32)
    d_rank = jnp.einsum("te,re->tr", d_step_low, step_back, preferred_element_type=jnp.float32)
    d_projected = jnp.concatenate(
        [d_rank, d_in_map.reshape(row_count, STATE), d_out_map.reshape(row_count, STATE)], axis=1
    ).astype(jnp.bfloat16)
    grad_proj = jnp.einsum("te,tk->ek", conv_low, d_projected, preferred_element_type=jnp.float32)
    d_conv = d_conv + jnp.einsum(
        "tk,ek->te", d_projected, proj_back, preferred_element_type=jnp.float32
    )
    d_conv_pre = d_conv * silu_slope(conv_pre)
    grad_conv_shift = jnp.sum(d_conv_pre, axis=0)
    grad_conv = jnp.stack(
        [
            jnp.sum(d_conv_pre * padded[offset : offset + row_count], axis=0)
            for offset in range(CONV)
        ]
    )
    padded_back = jnp.pad(d_conv_pre, ((0, CONV - 1), (0, 0)))
    d_inner = jnp.zeros_like(d_conv_pre)
    for offset in range(CONV):
        d_inner = (
            d_inner
            + taps_back[offset] * padded_back[CONV - 1 - offset : CONV - 1 - offset + row_count]
        )
    d_inner = d_inner.astype(jnp.bfloat16)
    grad_inner = jnp.einsum("td,te->de", normed, d_inner, preferred_element_type=jnp.float32)
    grad_gate = jnp.einsum("td,te->de", normed, d_gate, preferred_element_type=jnp.float32)
    d_normed = jnp.einsum("te,de->td", d_inner, inner_back, preferred_element_type=jnp.float32)
    d_normed = d_normed + jnp.einsum(
        "te,de->td", d_gate, gate_back, preferred_element_type=jnp.float32
    )
    grad_gain = jnp.sum(d_normed * residual * inv_rms, axis=0)
    d_scaled = d_normed * gain_back
    d_tokens = (
        d_out
        + inv_rms * d_scaled
        - residual
        * inv_rms
        * inv_rms
        * inv_rms
        * jnp.mean(d_scaled * residual, axis=1, keepdims=True)
    )
    gradients = (
        grad_gain,
        grad_inner,
        grad_gate,
        grad_conv,
        grad_conv_shift,
        grad_proj,
        grad_step,
        grad_step_shift,
        grad_log,
        grad_skip,
        grad_out,
    )
    owned = (
        lax.psum_scatter(
            gradients[0].astype(jnp.bfloat16), "shard", scatter_dimension=0, tiled=True
        ).astype(jnp.float32),
        lax.psum_scatter(
            gradients[1].astype(jnp.bfloat16), "shard", scatter_dimension=1, tiled=True
        ).astype(jnp.float32),
        lax.psum_scatter(
            gradients[2].astype(jnp.bfloat16), "shard", scatter_dimension=1, tiled=True
        ).astype(jnp.float32),
        lax.psum_scatter(
            gradients[3].astype(jnp.bfloat16), "shard", scatter_dimension=1, tiled=True
        ).astype(jnp.float32),
        lax.psum_scatter(
            gradients[4].astype(jnp.bfloat16), "shard", scatter_dimension=0, tiled=True
        ).astype(jnp.float32),
        lax.psum_scatter(
            gradients[5].astype(jnp.bfloat16), "shard", scatter_dimension=0, tiled=True
        ).astype(jnp.float32),
        lax.psum_scatter(
            gradients[6].astype(jnp.bfloat16), "shard", scatter_dimension=1, tiled=True
        ).astype(jnp.float32),
        lax.psum_scatter(
            gradients[7].astype(jnp.bfloat16), "shard", scatter_dimension=0, tiled=True
        ).astype(jnp.float32),
        lax.psum_scatter(
            gradients[8].astype(jnp.bfloat16), "shard", scatter_dimension=1, tiled=True
        ).astype(jnp.float32),
        lax.psum_scatter(
            gradients[9].astype(jnp.bfloat16), "shard", scatter_dimension=0, tiled=True
        ).astype(jnp.float32),
        lax.psum_scatter(
            gradients[10].astype(jnp.bfloat16), "shard", scatter_dimension=0, tiled=True
        ).astype(jnp.float32),
    )
    totals = (
        lax.psum(owned[0].astype(jnp.bfloat16), "replica").astype(jnp.float32),
        lax.psum(owned[1].astype(jnp.bfloat16), "replica").astype(jnp.float32),
        lax.psum(owned[2].astype(jnp.bfloat16), "replica").astype(jnp.float32),
        lax.psum(owned[3].astype(jnp.bfloat16), "replica").astype(jnp.float32),
        lax.psum(owned[4].astype(jnp.bfloat16), "replica").astype(jnp.float32),
        lax.psum(owned[5].astype(jnp.bfloat16), "replica").astype(jnp.float32),
        lax.psum(owned[6].astype(jnp.bfloat16), "replica").astype(jnp.float32),
        lax.psum(owned[7].astype(jnp.bfloat16), "replica").astype(jnp.float32),
        lax.psum(owned[8].astype(jnp.bfloat16), "replica").astype(jnp.float32),
        lax.psum(owned[9].astype(jnp.bfloat16), "replica").astype(jnp.float32),
        lax.psum(owned[10].astype(jnp.bfloat16), "replica").astype(jnp.float32),
    )
    return (output, d_tokens) + tuple(totals)


def solution(mesh):
    return jax.shard_map(
        local,
        mesh=mesh,
        in_specs=(
            P(("replica", "shard"), None),
            P("shard"),
            P(None, "shard"),
            P(None, "shard"),
            P(None, "shard"),
            P("shard"),
            P("shard", None),
            P(None, "shard"),
            P("shard"),
            P(None, "shard"),
            P("shard"),
            P("shard", None),
            P(("replica", "shard"), None),
            P(("replica", "shard")),
        ),
        out_specs=(
            P(("replica", "shard"), None),
            P(("replica", "shard"), None),
            P("shard"),
            P(None, "shard"),
            P(None, "shard"),
            P(None, "shard"),
            P("shard"),
            P("shard", None),
            P(None, "shard"),
            P("shard"),
            P(None, "shard"),
            P("shard"),
            P("shard", None),
        ),
        check_vma=False,
    )
```

profile of v0, /device:TPU:0, one launch (start us, length us, event | category | flops | bytes accessed | tf_op | source)
XLA Modules:
  0.0 1690.7 jit_solution(2680614008914937016)
XLA Ops:
  13.0 35.5 %all-reduce.39 = bf16[1024]{0:T(1024)(128)(2,1)S(1)} all-reduce(bf16[1024]{0:T(1024)(128)(2,1)S(1)} %dynamic-update-slice.24), channel_id=1, replica_groups=mesh['replica'=2,'shard'=16] {'shard'}, use_global_device_ids=true, to_apply=%add.39 | all-reduce | flops 1024 | bytes 4096
  48.5 17.3 %all-gather = bf16[16,1,128]{2,1,0:T(2,128)(2,1)S(1)} all-gather(bf16[1,1,128]{2,1,0:T(2,128)(2,1)} %bitcast.173), channel_id=1, replica_groups=mesh['replica'=2,'shard'=16] {'shard'}, dimensions={0}, use_global_device_ids=true | all-gather | bytes 4352 | tf_op jit(solution)/shard_map/all_gather | solution.py:84
  66.4 19.2 %all-gather.1 = bf16[16,1,128]{2,1,0:T(2,128)(2,1)S(1)} all-gather(bf16[1,1,128]{2,1,0:T(2,128)(2,1)} %bitcast.174), channel_id=1, replica_groups=mesh['replica'=2,'shard'=16] {'shard'}, dimensions={0}, use_global_device_ids=true | all-gather | bytes 4352 | tf_op jit(solution)/shard_map/all_gather | solution.py:87
  86.2 17.6 %all-gather.2 = bf16[16,1,128]{2,1,0:T(2,128)(2,1)S(1)} all-gather(bf16[1,1,128]{2,1,0:T(2,128)(2,1)} %bitcast.175), channel_id=1, replica_groups=mesh['replica'=2,'shard'=16] {'shard'}, dimensions={0}, use_global_device_ids=true | all-gather | bytes 4352 | tf_op jit(solution)/shard_map/all_gather | solution.py:89
  104.3 19.0 %all_gather.41 = bf16[4,2048]{1,0:T(4,128)(2,1)S(1)} all-gather(bf16[4,128]{1,0:T(4,128)(2,1)} %param.28), channel_id=1, replica_groups=mesh['replica'=2,'shard'=16] {'shard'}, dimensions={1}, use_global_device_ids=true | all-gather | bytes 17408 | tf_op jit(solution)/shard_map/all_gather | solution.py:83
  123.4 18.0 %all_gather.47 = bf16[16,2048]{1,0:T(8,128)(2,1)S(1)} all-gather(bf16[16,128]{1,0:T(8,128)(2,1)} %param.33), channel_id=1, replica_groups=mesh['replica'=2,'shard'=16] {'shard'}, dimensions={1}, use_global_device_ids=true | all-gather | bytes 69632 | tf_op jit(solution)/shard_map/all_gather | solution.py:88
  141.9 20.6 %all_gather.45 = bf16[64,2048]{1,0:T(8,128)(2,1)S(1)} all-gather(bf16[64,128]{1,0:T(8,128)(2,1)} %param.31), channel_id=1, replica_groups=mesh['replica'=2,'shard'=16] {'shard'}, dimensions={1}, use_global_device_ids=true | all-gather | bytes 278528 | tf_op jit(solution)/shard_map/all_gather | solution.py:86
  163.7 21.0 %all_gather.44 = bf16[2048,96]{0,1:T(8,128)(2,1)} all-gather(bf16[128,96]{0,1:T(8,128)(2,1)} %param.30), channel_id=1, replica_groups=mesh['replica'=2,'shard'=16] {'shard'}, dimensions={0}, use_global_device_ids=true | all-gather | bytes 417792 | tf_op jit(solution)/shard_map/all_gather | solution.py:85
  203.5 289.7 %while.44 = (s32[]{:T(128)}, f32[16,2048]{1,0:T(8,128)S(1)}, f32[2,16,2048]{2,1,0:T(8,128)}, f32[2,64,2048]{2,1,0:T(8,128)}, f32[2,64,2048]{2,1,0:T(8,128)S(1)},...) while((s32[]{:T(128)}, f32[16,2048]{1,0:T(8,128)S(1)}, ...), condition=%wide.region_2.3_spmd, body=%wide.region_1.2_spmd.sunk | while | flops 49446912 | bytes 403096384 | solution.py:135
  295.8 21.1 %pad.580 = f32[64,16,2048]{2,1,0:T(8,128)} pad(f32[32,16,2048]{2,1,0:T(8,128)} %pad_maximum_fusion.38, f32[]{:T(128)} %constant.207.clone.1..sunk), padding=0_1_1x0_0_0x0_0_0 | pad | bytes 12582916 | tf_op jit(solution)/shard_map/while/body/eval_jaxpr/pad | solution.py:31
  316.9 21.1 %pad.579 = f32[64,16,2048]{2,1,0:T(8,128)} pad(f32[32,16,2048]{2,1,0:T(8,128)} %add.998, f32[]{:T(128)} %constant.207.clone.1..sunk), padding=1_0_1x0_0_0x0_0_0 | pad | bytes 12582916 | tf_op jit(solution)/shard_map/while/body/eval_jaxpr/pad | solution.py:31
  440.5 21.1 %pad.580 = f32[64,16,2048]{2,1,0:T(8,128)} pad(f32[32,16,2048]{2,1,0:T(8,128)} %pad_maximum_fusion.38, f32[]{:T(128)} %constant.207.clone.1..sunk), padding=0_1_1x0_0_0x0_0_0 | pad | bytes 12582916 | tf_op jit(solution)/shard_map/while/body/eval_jaxpr/pad | solution.py:31
  461.6 21.1 %pad.579 = f32[64,16,2048]{2,1,0:T(8,128)} pad(f32[32,16,2048]{2,1,0:T(8,128)} %add.998, f32[]{:T(128)} %constant.207.clone.1..sunk), padding=1_0_1x0_0_0x0_0_0 | pad | bytes 12582916 | tf_op jit(solution)/shard_map/while/body/eval_jaxpr/pad | solution.py:31
  497.2 667.2 %while.45 = (s32[]{:T(128)}, f32[16,2048]{1,0:T(8,128)}, f32[16,2048]{1,0:T(8,128)}, f32[2,64,2048]{2,1,0:T(8,128)}, bf16[2,64,16]{2,1,0:T(8,128)(2,1)}, /*index...) while((s32[]{:T(128)}, f32[16,2048]{1,0:T(8,128)}, ...), condition=%wide.region_9.10_spmd.clone, body=%wide.region_3.9_spmd.clone.sunk | while | flops 83916800 | bytes 814883776 | solution.py:173
  623.5 21.0 %pad.616 = f32[64,16,2048]{2,1,0:T(8,128)} pad(f32[32,16,2048]{2,1,0:T(8,128)} %pad_maximum_fusion.43, f32[]{:T(128)} %constant.207.clone.1..sunk.1), padding=0_1_1x0_0_0x0_0_0 | pad | bytes 12582916 | tf_op jit(solution)/shard_map/while/body/eval_jaxpr/pad | solution.py:49
  644.4 21.1 %pad.615 = f32[64,16,2048]{2,1,0:T(8,128)} pad(f32[32,16,2048]{2,1,0:T(8,128)} %add.1027, f32[]{:T(128)} %constant.207.clone.1..sunk.1), padding=1_0_1x0_0_0x0_0_0 | pad | bytes 12582916 | tf_op jit(solution)/shard_map/while/body/eval_jaxpr/pad | solution.py:49
  759.3 21.1 %pad.626 = f32[64,16,2048]{2,1,0:T(8,128)} pad(f32[32,16,2048]{2,1,0:T(8,128)} %pad_maximum_fusion.48, f32[]{:T(128)} %constant.207.clone.1..sunk.1), padding=0_1_1x0_0_0x0_0_0 | pad | bytes 12582916 | tf_op jit(solution)/shard_map/while/body/eval_jaxpr/pad | solution.py:31
  780.4 21.1 %pad.625 = f32[64,16,2048]{2,1,0:T(8,128)} pad(f32[32,16,2048]{2,1,0:T(8,128)} %add.1032, f32[]{:T(128)} %constant.207.clone.1..sunk.1), padding=1_0_1x0_0_0x0_0_0 | pad | bytes 12582916 | tf_op jit(solution)/shard_map/while/body/eval_jaxpr/pad | solution.py:31
  820.2 15.0 add_reduce_fusion.2
  941.9 21.0 %pad.616 = f32[64,16,2048]{2,1,0:T(8,128)} pad(f32[32,16,2048]{2,1,0:T(8,128)} %pad_maximum_fusion.43, f32[]{:T(128)} %constant.207.clone.1..sunk.1), padding=0_1_1x0_0_0x0_0_0 | pad | bytes 12582916 | tf_op jit(solution)/shard_map/while/body/eval_jaxpr/pad | solution.py:49
  962.9 21.1 %pad.615 = f32[64,16,2048]{2,1,0:T(8,128)} pad(f32[32,16,2048]{2,1,0:T(8,128)} %add.1027, f32[]{:T(128)} %constant.207.clone.1..sunk.1), padding=1_0_1x0_0_0x0_0_0 | pad | bytes 12582916 | tf_op jit(solution)/shard_map/while/body/eval_jaxpr/pad | solution.py:49
  1077.8 21.1 %pad.626 = f32[64,16,2048]{2,1,0:T(8,128)} pad(f32[32,16,2048]{2,1,0:T(8,128)} %pad_maximum_fusion.48, f32[]{:T(128)} %constant.207.clone.1..sunk.1), padding=0_1_1x0_0_0x0_0_0 | pad | bytes 12582916 | tf_op jit(solution)/shard_map/while/body/eval_jaxpr/pad | solution.py:31
  1098.9 21.1 %pad.625 = f32[64,16,2048]{2,1,0:T(8,128)} pad(f32[32,16,2048]{2,1,0:T(8,128)} %add.1032, f32[]{:T(128)} %constant.207.clone.1..sunk.1), padding=1_0_1x0_0_0x0_0_0 | pad | bytes 12582916 | tf_op jit(solution)/shard_map/while/body/eval_jaxpr/pad | solution.py:31
  1138.6 15.0 add_reduce_fusion.2
  1220.6 59.4 %all-reduce.44 = (bf16[1024]{0:T(1024)(128)(2,1)S(1)}, bf16[2048]{0:T(1024)(128)(2,1)S(1)}, bf16[2048]{0:T(1024)(128)(2,1)S(1)}, bf16[2048]{0:T(1024)(128)(2,1)S(1)}) all-reduce(bf16[1024]{0:T(1024)(128)(2,1)S(1)} %get-tuple-element.551, ...), channel_id=2, replica_groups=mesh['replica'=2,'shard'=16] {'shard'}, use_global_device_ids=true, to_apply=%region_12.13.clone | all-reduce | flops 7168 | bytes 28672
  1282.1 49.2 %reduce-scatter.24.cloned.1.call-done = bf16[128,1024]{1,0:T(8,128)(2,1)} async-done(((bf16[2048,1024]{1,0:T(8,128)(2,1)}), bf16[128,1024]{1,0:T(8,128)(2,1)}) %reduce-scatter.24.cloned.1.call-update) | async-done | bytes 262160
  1333.1 73.4 %reduce-scatter.20.cloned.1.call-done = bf16[128,1024]{1,0:T(8,128)(2,1)} async-done(((bf16[2048,1024]{1,0:T(8,128)(2,1)}), bf16[128,1024]{1,0:T(8,128)(2,1)}) %reduce-scatter.20.cloned.1.call-update) | async-done | bytes 262160 | tf_op jit(solution)/shard_map/reduce_scatter | solution.py:277
  1411.1 54.6 %reduce-scatter.26.cloned.1.call-done = bf16[128,4]{1,0:T(8,128)(2,1)} async-done(((bf16[2048,4]{1,0:T(8,128)(2,1)}), bf16[128,4]{1,0:T(8,128)(2,1)}) %reduce-scatter.26.cloned.1.call-update) | async-done | bytes 1040
  1466.6 57.6 %reduce-scatter.32.cloned.1.call-done = bf16[128,16]{1,0:T(8,128)(2,1)} async-done(((bf16[2048,16]{1,0:T(8,128)(2,1)}), bf16[128,16]{1,0:T(8,128)(2,1)}) %reduce-scatter.32.cloned.1.call-update) | async-done | bytes 4112
  1525.0 58.6 %reduce-scatter.30.cloned.1.call-done = bf16[128,64]{1,0:T(8,128)(2,1)} async-done(((bf16[2048,64]{1,0:T(8,128)(2,1)}), bf16[128,64]{1,0:T(8,128)(2,1)}) %reduce-scatter.30.cloned.1.call-update) | async-done | bytes 16400
  1584.4 58.0 %reduce-scatter.28.cloned.1.call-done = bf16[128,96]{1,0:T(8,128)(2,1)} async-done(((bf16[2048,96]{1,0:T(8,128)(2,1)}), bf16[128,96]{1,0:T(8,128)(2,1)}) %reduce-scatter.28.cloned.1.call-update) | async-done | bytes 24592
  1656.6 22.0 %all-reduce.49.cloned.1.call-done = (bf16[1024,128]{1,0:T(8,128)(2,1)}, bf16[1024,128]{1,0:T(8,128)(2,1)}, bf16[128,1024]{1,0:T(8,128)(2,1)}) async-done(((bf16[1024,128]{1,0:T(8,128)(2,1)}, bf16[1024,128]{1,0:T(8,128)(2,1)}, bf16[128,1024]{1,0:T(8,128)(2,1)}), (bf16[1024,128]{1,0:T(8,128)(2,1)}, bf16[1024,128]{1,0:T(8,128)(2,1)}, bf16[128,1024]{1,0:T(8,128)(2,1)})) %all-reduce.49.cloned.1.call-update) | async-done | bytes 786448 | tf_op jit(solution)/shard_map/psum | solution.py:283
  (717 shorter events, 757.3 us)
Async XLA Ops:
  7.2 181.3 %copy-start.47 = (bf16[128,1024]{1,0:T(8,128)(2,1)S(1)}, bf16[128,1024]{1,0:T(8,128)(2,1)}, u32[]{:S(2)}) copy-start(bf16[128,1024]{1,0:T(8,128)(2,1)} %param.24) | copy-start | bytes 786436
  7.2 178.2 %all-gather.9.cloned.1.call-start = ((), (), s32[]{:S(2)}) async-start(), calls=%async_computation.8 | async-start | bytes 4456448 | tf_op jit(solution)/shard_map/all_gather | solution.py:82
  7.9 180.5 %all-gather.7.cloned.1.call-start = ((), (), s32[]{:S(2)}) async-start(), calls=%async_computation.7 | async-start | bytes 4456448 | tf_op jit(solution)/shard_map/all_gather | solution.py:81
  8.7 183.2 %all-gather.11.cloned.1.call-start = ((), (), s32[]{:S(2)}) async-start(), calls=%async_computation.9 | async-start | bytes 4456448 | tf_op jit(solution)/shard_map/all_gather | solution.py:90
  9.4 1270.9 %reduce-scatter.22.cloned.1.call-start = ((), (), s32[]{:S(2)}) async-start(), calls=%async_computation.11 | async-start | bytes 4456448
  48.5 143.3 %copy-start.80 = (f32[1024]{0:T(1024)}, f32[1024]{0:T(1024)S(1)}, u32[]{:S(2)}) copy-start(f32[1024]{0:T(1024)S(1)} %convert_element_type.153) | copy-start | bytes 12292
  141.4 50.4 %copy-start.84 = (bf16[16,2048]{1,0:T(8,128)(2,1)}, bf16[16,2048]{1,0:T(8,128)(2,1)S(1)}, u32[]{:S(2)}) copy-start(bf16[16,2048]{1,0:T(8,128)(2,1)S(1)} %all_gather.47) | copy-start | bytes 196612
  162.5 37.5 %copy-start.75 = (bf16[64,2048]{1,0:T(8,128)(2,1)}, bf16[64,2048]{1,0:T(8,128)(2,1)S(1)}, u32[]{:S(2)}) copy-start(bf16[64,2048]{1,0:T(8,128)(2,1)S(1)} %all_gather.45) | copy-start | bytes 786436
  316.9 22.1 %copy-start.74 = (f32[64,16,1]{1,2,0:T(1,128)S(1)}, f32[64,16,1]{1,2,0:T(1,128)}, u32[]{:S(2)}) copy-start(f32[64,16,1]{1,2,0:T(1,128)} %copy.63) | copy-start | bytes 12292 | tf_op jit(solution)/shard_map/while
  461.6 22.1 %copy-start.74 = (f32[64,16,1]{1,2,0:T(1,128)S(1)}, f32[64,16,1]{1,2,0:T(1,128)}, u32[]{:S(2)}) copy-start(f32[64,16,1]{1,2,0:T(1,128)} %copy.63) | copy-start | bytes 12292 | tf_op jit(solution)/shard_map/while
  780.4 21.1 %copy-start.38 = (f32[64,2048]{1,0:T(8,128)S(1)}, f32[64,2048]{1,0:T(8,128)}, u32[]{:S(2)}) copy-start(f32[64,2048]{1,0:T(8,128)} %copy-done.37) | copy-start | bytes 1572868 | tf_op jit(solution)/shard_map/while
  820.1 15.2 copy-start.86
  820.1 15.2 copy-start.68
  820.1 15.2 copy-start.70
  820.1 16.6 copy-start.42
  820.1 16.6 copy-start.46
  820.1 16.6 copy-start.83
  1098.9 21.1 %copy-start.38 = (f32[64,2048]{1,0:T(8,128)S(1)}, f32[64,2048]{1,0:T(8,128)}, u32[]{:S(2)}) copy-start(f32[64,2048]{1,0:T(8,128)} %copy-done.37) | copy-start | bytes 1572868 | tf_op jit(solution)/shard_map/while
  1138.5 15.2 copy-start.68
  1138.6 15.2 copy-start.70
  1138.6 16.6 copy-start.42
  1138.6 16.6 copy-start.46
  1138.6 16.6 copy-start.83
  1184.2 147.1 %reduce-scatter.24.cloned.1.call-start = ((), (), s32[]{:S(2)}) async-start(), calls=%async_computation.12 | async-start | bytes 4456448
  1194.2 212.2 %reduce-scatter.20.cloned.1.call-start = ((), (), s32[]{:S(2)}) async-start(), calls=%async_computation.10 | async-start | bytes 4456448 | tf_op jit(solution)/shard_map/reduce_scatter | solution.py:277
  1199.2 266.5 %reduce-scatter.26.cloned.1.call-start = ((), (), s32[]{:S(2)}) async-start(), calls=%async_computation.13 | async-start | bytes 557056
  1204.5 319.7 %reduce-scatter.32.cloned.1.call-start = ((), (), s32[]{:S(2)}) async-start(), calls=%async_computation.16 | async-start | bytes 557056
  1207.9 375.6 %reduce-scatter.30.cloned.1.call-start = ((), (), s32[]{:S(2)}) async-start(), calls=%async_computation.15 | async-start | bytes 557056
  1211.6 430.7 %reduce-scatter.28.cloned.1.call-start = ((), (), s32[]{:S(2)}) async-start(), calls=%async_computation.14 | async-start | bytes 557056
  1215.0 463.6 %all-reduce.49.cloned.1.call-start = ((), (), s32[]{:S(2)}) async-start(), calls=%async_computation.17 | async-start | bytes 1572864 | tf_op jit(solution)/shard_map/psum | solution.py:283
  1219.0 187.5 %copy-start.79 = (bf16[128,1024]{1,0:T(8,128)(2,1)S(1)}, bf16[128,1024]{1,0:T(8,128)(2,1)}, u32[]{:S(2)}) copy-start(bf16[128,1024]{1,0:T(8,128)(2,1)} %param.36) | copy-start | bytes 786436
  1219.0 188.6 %copy-start.105 = (f32[128]{0:T(128)S(1)}, f32[128]{0:T(128)}, u32[]{:S(2)}) copy-start(f32[128]{0:T(128)} %compare_convert_fusion) | copy-start | bytes 1540
  (159 other events, 766.8 us)
Sparse Core Ops, SparseCore 0:
  10.2 55.9 all-gather.8
  68.3 51.5 all-gather.6
  122.0 51.5 all-gather.10
  1184.3 71.1 reduce-scatter.21
  1259.7 71.5 reduce-scatter.23
  1335.0 71.3 reduce-scatter.19
  1411.0 54.7 reduce-scatter.25
  1469.3 54.8 reduce-scatter.31
  1528.7 54.7 reduce-scatter.29
  1587.5 54.7 reduce-scatter.27
  1644.9 33.7 all-reduce.48
where the time goes:
time: 1710 us; the launch traced here: 1690 us
  local copies, waits for them, and re-layouts  580 us (34%)
  other arithmetic  390 us (23%)
  waiting for transfers between devices  376 us (22%)
  blocking collectives  236 us (14%)
  matrix products  57.8 us (3%)
  loops' own time  32.6 us (2%)
  between operations  17.2 us (1%)
    pad x40, local copies, waits for them, and re-layouts, block_states(): states = lax.associative_scan(combine, (decays, driven), axis=0)[1]  308 us
    unnamed x17, waiting for transfers between devices  280 us
    pad x20, local copies, waits for them, and re-layouts, scan_backward(): lax.associative_scan(combine, (shifted[::-1], d_states[::-1]), axis=0)[1]  154 us
    unnamed x2, blocking collectives  94.9 us
    add x30, other arithmetic, combine(): return (earlier[0] * later[0], later[0] * earlier[1] + later[1])  89.1 us
    mul x24, other arithmetic, combine(): return (earlier[0] * later[0], later[0] * earlier[1] + later[1])  86.2 us
    reduce_scatter x1, waiting for transfers between devices, local(): lax.psum_scatter(gradients[10].astype(jnp.bfloat16), 'shard', scatter_dim...  73.4 us
    add x22, other arithmetic, block_states(): states = lax.associative_scan(combine, (decays, driven), axis=0)[1]  49.6 us
  transfers between devices with their start and end apart: 11, of which 7 were waited for; matrix products, arithmetic and copies ran while one was open for 4% of the time, Pallas kernels for 0%

commit v1 on v0

v1 whole, which is shorter than its diff:
```python
import functools
import math
from types import SimpleNamespace

import jax
import jax.numpy as jnp
from jax import lax
from jax.experimental import pallas as pl
from jax.experimental.pallas import tpu as pltpu
from jax.sharding import PartitionSpec as P

RANK = 64
STATE = 16
CONV = 4
SLOT = 128
EPS = 1e-05
LN2 = math.log(2.0)
PACK = 96
MESH = pl.DeviceIdType.MESH
F32 = jnp.float32
BF16 = jnp.bfloat16


def nt(left, right):
    return lax.dot_general(left, right, (((1,), (1,)), ((), ())), preferred_element_type=F32)


def nn(left, right):
    return lax.dot_general(left, right, (((1,), (0,)), ((), ())), preferred_element_type=F32)


def tn(left, right):
    return lax.dot_general(left, right, (((0,), (0,)), ((), ())), preferred_element_type=F32)


def buffers(depth, hl, width, shards, piece):
    cols = depth * hl
    rows = 8 * SLOT
    reduce_small = dict(
        s1=((4, SLOT, 128), BF16),
        l1=((4, SLOT, 128), BF16),
        s2=((4, SLOT, 128), BF16),
        l2=((4, SLOT, 128), BF16),
        s3=((4, SLOT, 128), BF16),
        l3=((4, SLOT, 128), BF16),
        own=((4, SLOT, 128), F32),
        oth=((4, SLOT, 128), F32),
    )
    reduce_large = dict(
        s1=((4, SLOT, width), BF16),
        l1=((4, SLOT, width), BF16),
        sx=((2, SLOT // 2, width), BF16),
        sy=((2, SLOT // 2, width), BF16),
        lx=((2, SLOT // 2, width), BF16),
        ly=((2, SLOT // 2, width), BF16),
        tx=((SLOT // 2, width), BF16),
        ty=((SLOT // 2, width), BF16),
        mx=((SLOT // 2, width), BF16),
        my=((SLOT // 2, width), BF16),
    )
    shapes = dict(
        wt=((3, depth, hl, width), BF16),
        ws=((2, cols, width), BF16),
        pka=((depth, PACK, 128), BF16),
        wpa=((depth, hl, 128), BF16),
        gb=((depth, 2, 2, 8, 128), F32),
        gl=((1, width), F32),
        nb=((4, 2, SLOT, width), BF16),
        db=((4, 2, SLOT, width), BF16),
        pkl=((PACK, cols), F32),
        wst=((128, cols), BF16),
        rate=((STATE, 2, 8, 128), F32),
        ip=((8, SLOT + 8, cols), F32),
        dcp=((SLOT + 8, cols), F32),
        tm=((rows, 128), F32),
        spread=((rows, 256), BF16),
        sel=((256, 2 * STATE * 128), BF16),
        bc=((SLOT, 2 * STATE, 8, 128), F32),
        sall=((SLOT + 2, STATE, 16, 128), BF16),
        cl=((8, SLOT, cols), BF16),
        xc=((2, rows, 128), F32),
        pp=((4, 2, SLOT, 128), F32),
        slow=((rows, 128), BF16),
        dpj=((rows, 128), BF16),
        dt=((2, rows, 128), F32),
        ys=((2, rows, 128), F32),
        dm=((2, rows, 128), F32),
        ga=((STATE, 2, 8, 128), F32),
        go=((4, 2, SLOT, cols), BF16),
        dg=((4, 2, SLOT, cols), BF16),
        di=((4, 2, SLOT, cols), BF16),
        dsl=((8, SLOT, cols), BF16),
        tt=((cols, rows), BF16),
        gws=((3, depth, hl, width), BF16),
        gwl=((3, depth - 1, hl, width), BF16),
        gys=((3, hl, width), BF16),
        gyl=((3, hl, width), BF16),
        sg=((PACK, cols), F32),
        sgs=((depth, PACK, 128), BF16),
        sgl=((depth - 1, PACK, 128), BF16),
        sgt=((PACK, 128), BF16),
        sgy=((PACK, 128), BF16),
        gps=((depth, hl, 128), BF16),
        gpl=((depth - 1, hl, 128), BF16),
        gpt=((hl, 128), BF16),
        gpy=((hl, 128), BF16),
        vv=((1, width), F32),
        sum=((4, SLOT, width), F32),
        vs=((4, 8, 128), F32),
        vl=((3, 8, 128), F32),
        vz=((depth - 1, 8, 128), F32),
    )
    return [shapes, reduce_small, reduce_small, reduce_large]


def main_kernel(names, depth, hl, piece, nsem, *refs):
    (tok, cot, win, wg, wo, wp, pk, gain, lens, bsum, dsc, gout, sout, pout, vout) = refs[:15]
    send_sems, recv_sems = refs[-2:]
    sets, at = [], 15
    for group in names:
        sets.append(SimpleNamespace(**dict(zip(group, refs[at:]))))
        at += len(group)
    b = sets[0]
    width = tok.shape[1]
    cols = depth * hl
    el = 2 * hl

    r = lax.axis_index("replica")
    s = lax.axis_index("shard")
    y = lax.rem(r, 2)
    f = s // 4
    x = lax.rem(s // 2, 2)
    c = lax.rem(s, 2)
    core = (r, s + 1 - 2 * c)
    xpeer = (r, s + 2 - 4 * x)
    ypeer = (r + 1 - 2 * y, s)
    zpos = [lax.rem(f + k, depth) for k in range(1, depth)]
    zpeers = [(r, s + 4 * (q - f)) for q in zpos]
    q0 = y * 2 + x
    qx = y * 2 + 1 - x
    qy = (1 - y) * 2 + x
    qd = (1 - y) * 2 + 1 - x
    oc = 1 - c
    half = SLOT // 2

    counter = [0]
    started = []

    def rcopy(src, dst, dev):
        i = counter[0]
        counter[0] += 1
        assert i < nsem
        cp = pltpu.make_async_remote_copy(
            src_ref=src,
            dst_ref=dst,
            send_sem=send_sems.at[i],
            recv_sem=recv_sems.at[i],
            device_id=dev,
            device_id_type=MESH,
        )
        cp.start()
        started.append(cp)
        return cp

    def settle(cps):
        for cp in cps:
            cp.wait_send()
            started[:] = [other for other in started if other is not cp]

    barrier = pltpu.get_barrier_semaphore()
    for dev in [core, xpeer, ypeer] + zpeers:
        pl.semaphore_signal(barrier, inc=1, device_id=dev, device_id_type=MESH)

    b.gb[f, x, c] = gain[...]
    b.pka[f] = pk[...]
    wpv = wp[pl.ds(y * hl, hl), :].astype(F32)
    b.wpa[f] = jnp.concatenate([wpv, jnp.zeros((hl, 128 - wpv.shape[1]), F32)], axis=1).astype(BF16)
    wint = win[...].T
    b.wt[0, f] = jnp.where(y == 0, wint[:hl], wint[hl:])
    t32 = tok[...].astype(F32)
    inv = lax.rsqrt(jnp.mean(t32 * t32, axis=1, keepdims=True) + EPS)
    b.nb[q0, c] = (t32 * inv).astype(BF16)

    pl.semaphore_wait(barrier, 2 + depth)

    gcore = rcopy(b.gb.at[f, x, c], b.gb.at[f, x, c], core)

    def plane_start(buf):
        ax = rcopy(buf.at[q0, c, pl.ds(0, half)], buf.at[q0, c, pl.ds(0, half)], xpeer)
        by = rcopy(buf.at[q0, c, pl.ds(half, half)], buf.at[q0, c, pl.ds(half, half)], ypeer)
        bx = rcopy(buf.at[q0, c, pl.ds(half, half)], buf.at[q0, c, pl.ds(half, half)], xpeer)
        ay = rcopy(buf.at[q0, c, pl.ds(0, half)], buf.at[q0, c, pl.ds(0, half)], ypeer)
        oo = rcopy(buf.at[q0, c], buf.at[q0, c], core)
        return ax, by, bx, ay, oo

    def plane_forward(buf, cps):
        ax, by, bx, ay, oo = cps
        ax.wait_recv()
        fa = rcopy(buf.at[qx, c, pl.ds(0, half)], buf.at[qx, c, pl.ds(0, half)], ypeer)
        by.wait_recv()
        fb = rcopy(buf.at[qy, c, pl.ds(half, half)], buf.at[qy, c, pl.ds(half, half)], xpeer)
        bx.wait_recv()
        ox = rcopy(buf.at[qx, c], buf.at[qx, c], core)
        ay.wait_recv()
        oy = rcopy(buf.at[qy, c], buf.at[qy, c], core)
        return oo, ox, oy, fa, fb

    def plane_finish(buf, cps):
        oo, ox, oy, fa, fb = cps
        fa.wait_recv()
        fb.wait_recv()
        od = rcopy(buf.at[qd, c], buf.at[qd, c], core)
        oo.wait_recv()
        ox.wait_recv()
        oy.wait_recv()
        od.wait_recv()

    nstart = plane_start(b.nb)
    zsmall = [rcopy(b.pka.at[f], b.pka.at[f], dev) for dev in zpeers]
    zsmall += [rcopy(b.wpa.at[f], b.wpa.at[f], dev) for dev in zpeers]
    zin = [rcopy(b.wt.at[0, f], b.wt.at[0, f], dev) for dev in zpeers]

    gcore.wait_recv()
    gx = rcopy(b.gb.at[f, x], b.gb.at[f, x], xpeer)
    wgt = wg[...].T
    b.wt[1, f] = jnp.where(y == 0, wgt[:hl], wgt[hl:])
    b.wt[2, f] = wo[pl.ds(y * hl, hl), :]
    rowid = lax.broadcasted_iota(jnp.int32, (SLOT, 1), 0)
    b.db[q0, c] = jnp.where(rowid < lens[0], cot[...].astype(F32), 0.0).astype(BF16)
    b.ip[:, 0:8, :] = jnp.zeros((8, 8, cols), F32)
    b.dcp[SLOT : SLOT + 8, :] = jnp.zeros((8, cols), F32)
    b.ga[...] = jnp.zeros((STATE, 2, 8, 128), F32)
    b.sall[1] = jnp.zeros((STATE, 16, 128), BF16)
    source = lax.broadcasted_iota(jnp.int32, (256, 2 * STATE * 128), 0)
    target = lax.broadcasted_iota(jnp.int32, (256, 2 * STATE * 128), 1)
    b.sel[...] = jnp.where(lax.rem(source, 128) == RANK + target // 128, 1.0, 0.0).astype(BF16)
    gx.wait_recv()
    gz = [rcopy(b.gb.at[f], b.gb.at[f], dev) for dev in zpeers]

    nmid = plane_forward(b.nb, nstart)
    for cp in gz + zsmall:
        cp.wait_recv()
    pieces = []
    for i in range(depth):
        for j in range(2):
            for k in range(2):
                pieces.append(b.gb[i, j, k][0:1, :piece])
    gl = jnp.concatenate(pieces, axis=1)
    b.gl[...] = gl
    locs = []
    for i in range(depth):
        full = b.pka[i].astype(F32)
        locs.append(jnp.where(y == 0, full[:, :hl], full[:, hl:el]))
    pkl = jnp.concatenate(locs, axis=1)
    b.pkl[...] = pkl
    b.wst[...] = jnp.concatenate([pkl[:RANK], jnp.zeros((128 - RANK, cols), F32)], axis=0).astype(BF16)
    for n in range(STATE):
        row = -jnp.exp(pkl[RANK + n : RANK + n + 1]) * (1.0 / LN2)
        for et in range(2):
            b.rate[n, et] = jnp.broadcast_to(row[:, et * 128 : et * 128 + 128], (8, 128))
    plane_finish(b.nb, nmid)
    dstart = plane_start(b.db)
    for cp in zin:
        cp.wait_recv()
    zgate = [rcopy(b.wt.at[1, f], b.wt.at[1, f], dev) for dev in zpeers]
    zout = [rcopy(b.wt.at[2, f], b.wt.at[2, f], dev) for dev in zpeers]

    def scaled(w):
        full = b.wt[w].reshape(cols, width).astype(F32)
        b.ws[w] = (full * b.gl[...]).astype(BF16)

    scaled(0)
    o = RANK + STATE
    taps = [b.pkl[o + k : o + k + 1, :] for k in range(CONV)]
    cbias = b.pkl[o + CONV : o + CONV + 1, :]
    sbias = b.pkl[o + CONV + 1 : o + CONV + 2, :]
    skip = b.pkl[o + CONV + 2 : o + CONV + 3, :]

    @pl.loop(0, 4)
    def _(q):
        pre = nt(b.nb[q].reshape(2 * SLOT, width), b.ws[0])
        b.ip[2 * q, 8 : 8 + SLOT, :] = pre[:SLOT]
        b.ip[2 * q + 1, 8 : 8 + SLOT, :] = pre[SLOT:]

    wpl = b.wpa[...].reshape(cols, 128)

    @pl.loop(0, 4)
    def _(q):
        for cc in range(2):
            j = 2 * q + cc
            acc = jnp.broadcast_to(cbias, (SLOT, cols))
            for k in range(CONV):
                acc = acc + taps[k] * b.ip[j, 5 + k : 5 + k + SLOT, :]
            out = acc * jax.nn.sigmoid(acc)
            rows = pl.ds(pl.multiple_of(j * SLOT, SLOT), SLOT)
            b.xc[0, rows, :] = out[:, :128]
            b.xc[1, rows, :] = out[:, 128:]
            low = out.astype(BF16)
            b.cl[j] = low
            b.pp[q, cc] = nn(low, wpl)

    def all_reduce(which, between):
        g = sets[which]
        g.s1[...] = b.pp[:, oc].astype(BF16)
        one = rcopy(g.s1, g.l1, core)
        between(0)
        one.wait_recv()
        total = b.pp[:, c] + g.l1[...].astype(F32)
        g.s2[...] = total.astype(BF16)
        two = [
            rcopy(g.s2.at[pl.ds(0, 2)], g.l2.at[pl.ds(0, 2)], xpeer),
            rcopy(g.s2.at[pl.ds(2, 2)], g.l2.at[pl.ds(2, 2)], ypeer),
        ]
        g.own[...] = total
        between(1)
        for cp in two:
            cp.wait_recv()
        total = g.own[...] + g.l2[...].astype(F32)
        g.s3[...] = total.astype(BF16)
        three = [
            rcopy(g.s3.at[pl.ds(0, 2)], g.l3.at[pl.ds(0, 2)], ypeer),
            rcopy(g.s3.at[pl.ds(2, 2)], g.l3.at[pl.ds(2, 2)], xpeer),
        ]
        g.own[...] = total
        between(2)
        for cp in three:
            cp.wait_recv()
        g.own[...] = g.own[...] + g.l3[...].astype(F32)
        four = rcopy(g.own, g.oth, core)
        between(3)
        four.wait_recv()

    dstate = [None]

    def pump_first(stage):
        if stage == 1:
            dstate[0] = plane_forward(b.db, dstart)
        if stage == 2:
            plane_finish(b.db, dstate[0])

    all_reduce(1, pump_first)

    @pl.loop(0, 4)
    def _(q):
        for cc, src in ((c, sets[1].own), (oc, sets[1].oth)):
            j = 2 * q + cc
            rows = pl.ds(pl.multiple_of(j * SLOT, SLOT), SLOT)
            proj = src[q]
            b.tm[pl.ds(j, SLOT, stride=8), :] = proj
            low = proj.astype(BF16)
            b.slow[rows, :] = low
            pre = nn(low, b.wst[...]) + sbias
            size = jnp.maximum(pre, 0.0) + jnp.log1p(jnp.exp(-jnp.abs(pre)))
            b.dt[0, rows, :] = size[:, :128]
            b.dt[1, rows, :] = size[:, 128:]

    tm = b.tm[...]
    high = tm.astype(BF16)
    spread = jnp.concatenate([high, (tm - high.astype(F32)).astype(BF16)], axis=1)
    b.spread[...] = spread

    @pl.loop(0, STATE)
    def _(i):
        chunk = pl.ds(pl.multiple_of(i * 256, 256), 256)
        both = nn(b.spread[...], b.sel[:, chunk])
        b.bc[:, 2 * i] = both[:, :128].reshape(SLOT, 8, 128)
        b.bc[:, 2 * i + 1] = both[:, 128:].reshape(SLOT, 8, 128)

    def forward_step(t, carry):
        at = pl.ds(t, 8, stride=SLOT)
        size = [b.dt[e, at, :] for e in range(2)]
        push = [size[e] * b.xc[e, at, :] for e in range(2)]
        out = [jnp.zeros((8, 128), F32) for _ in range(2)]
        new = []
        for n in range(STATE):
            inm = b.bc[t, n]
            outm = b.bc[t, STATE + n]
            for e in range(2):
                decay = jnp.exp2(size[e] * b.rate[n, e])
                state = decay * carry[2 * n + e] + push[e] * inm
                out[e] = out[e] + outm * state
                new.append(state)
            b.sall[t + 2, n] = jnp.concatenate(new[-2:], axis=0).astype(BF16)
        for e in range(2):
            b.ys[e, at, :] = out[e]
        return tuple(new)

    zero = jnp.zeros((8, 128), F32)
    lax.fori_loop(0, SLOT, forward_step, tuple(zero for _ in range(2 * STATE)))

    for cp in zgate:
        cp.wait_recv()
    scaled(1)
    for cp in zout:
        cp.wait_recv()
    wout = b.wt.at[2]
    b.sg[...] = jnp.zeros((PACK, cols), F32)
    skip_row = o + CONV + 2

    @pl.loop(0, 4)
    def _(q):
        gpre = nt(b.nb[q].reshape(2 * SLOT, width), b.ws[1])
        dgat = nt(b.db[q].reshape(2 * SLOT, width), wout[...].reshape(cols, width))
        rows = pl.ds(pl.multiple_of(q * 2 * SLOT, 2 * SLOT), 2 * SLOT)
        conv = jnp.concatenate([b.xc[0, rows, :], b.xc[1, rows, :]], axis=1)
        mixed = jnp.concatenate([b.ys[0, rows, :], b.ys[1, rows, :]], axis=1) + skip * conv
        sig = jax.nn.sigmoid(gpre)
        act = gpre * sig
        b.go[q] = (mixed * act).astype(BF16).reshape(2, SLOT, cols)
        dmix = dgat * act
        b.dm[0, rows, :] = dmix[:, :128]
        b.dm[1, rows, :] = dmix[:, 128:]
        slope = sig * (1.0 + gpre * (1.0 - sig))
        b.dg[q] = (dgat * mixed * slope).astype(BF16).reshape(2, SLOT, cols)
        b.sg[skip_row : skip_row + 1, :] += jnp.sum(dmix * conv, axis=0, keepdims=True)

    def reduce_begin(which, dots):
        g = sets[which]

        @pl.loop(0, width // 256)
        def _(i):
            chunk = pl.ds(pl.multiple_of(i * 256, 256), 256)
            g.s1[:, :, chunk] = dots(oc, chunk).astype(BF16).reshape(4, SLOT, 256)

        one = rcopy(g.s1, g.l1, core)

        @pl.loop(0, width // 256)
        def _(i):
            chunk = pl.ds(pl.multiple_of(i * 256, 256), 256)
            b.sum[:, :, chunk] = dots(c, chunk).reshape(4, SLOT, 256)

        return one

    def reduce_second(which, one):
        g = sets[which]
        one.wait_recv()
        top, low = slice(0, half), slice(half, SLOT)
        for k, q in ((0, qx), (1, qd)):
            g.sx[k] = (b.sum[q, top, :] + g.l1[q, top, :].astype(F32)).astype(BF16)
        cx = rcopy(g.sx, g.lx, xpeer)
        for k, q in ((0, qy), (1, qd)):
            g.sy[k] = (b.sum[q, low, :] + g.l1[q, low, :].astype(F32)).astype(BF16)
        cy = rcopy(g.sy, g.ly, ypeer)
        return cx, cy

    def reduce_third(which, cps):
        g = sets[which]
        cx, cy = cps
        top, low = slice(0, half), slice(half, SLOT)
        cx.wait_recv()
        g.ty[...] = (
            b.sum[qy, top, :] + g.l1[qy, top, :].astype(F32) + g.lx[1].astype(F32)
        ).astype(BF16)
        c1 = rcopy(g.ty, g.my, ypeer)
        cy.wait_recv()
        g.tx[...] = (
            b.sum[qx, low, :] + g.l1[qx, low, :].astype(F32) + g.ly[1].astype(F32)
        ).astype(BF16)
        c2 = rcopy(g.tx, g.mx, xpeer)
        return c1, c2

    def reduce_end(which, cps, out):
        g = sets[which]
        top, low = slice(0, half), slice(half, SLOT)
        for cp in cps:
            cp.wait_recv()
        out[top, :] = (
            b.sum[q0, top, :]
            + g.l1[q0, top, :].astype(F32)
            + g.lx[0].astype(F32)
            + g.my[...].astype(F32)
        )
        out[low, :] = (
            b.sum[q0, low, :]
            + g.l1[q0, low, :].astype(F32)
            + g.ly[0].astype(F32)
            + g.mx[...].astype(F32)
        )

    def weight_grad(w, lhs, rhs, gained, first):
        b.tt[...] = lhs[...].reshape(8 * SLOT, cols).T

        @pl.loop(0, width // 256)
        def _(i):
            chunk = pl.ds(pl.multiple_of(i * 256, 256), 256)
            grad = nn(b.tt[...], rhs[:, :, :, chunk].reshape(8 * SLOT, 256))
            if gained:
                part = jnp.sum(
                    grad * b.wt[w, :, :, chunk].reshape(cols, 256).astype(F32), axis=0, keepdims=True
                )
                if first:
                    b.vv[:, chunk] = part
                else:
                    b.vv[:, chunk] += part
                grad = grad * b.gl[:, chunk]
            b.gws[w, :, :, chunk] = grad.astype(BF16).reshape(depth, hl, 256)

        return [rcopy(b.gws.at[w, q], b.gwl.at[w, k], dev) for k, (q, dev) in enumerate(zip(zpos, zpeers))]

    def weight_sum(w, cps):
        total = b.gws[w, f].astype(F32)
        for k, cp in enumerate(cps):
            cp.wait_recv()
            total = total + b.gwl[w, k].astype(F32)
        gout[w, y] = total
        b.gys[w] = total.astype(BF16)
        return rcopy(b.gys.at[w], b.gyl.at[w], ypeer)

    bone = reduce_begin(
        3,
        lambda cc, chunk: nn(
            b.go[:, cc].reshape(4 * SLOT, cols), b.wt[2, :, :, chunk].reshape(cols, 256)
        ),
    )
    zgo = weight_grad(2, b.go, b.db, False, False)
    btwo = reduce_second(3, bone)
    zgg = weight_grad(1, b.dg, b.nb, True, True)

    def backward_one(t, carry):
        at = pl.ds(t, 8, stride=SLOT)
        size = [b.dt[e, at, :] for e in range(2)]
        conv = [b.xc[e, at, :] for e in range(2)]
        dmix = [b.dm[e, at, :] for e in range(2)]
        push = [size[e] * conv[e] for e in range(2)]
        rate_sum = [zero, zero]
        weighted = [zero, zero]
        new, dins, douts = [], [], []
        for n in range(STATE):
            inm = b.bc[t, n]
            outm = b.bc[t, STATE + n]
            before = b.sall[t + 1, n].astype(F32)
            after = b.sall[t + 2, n].astype(F32)
            din = zero
            dout = zero
            for e in range(2):
                rate = b.rate[n, e]
                decay = jnp.exp2(size[e] * rate)
                lam = outm * dmix[e] + carry[2 * n + e]
                back = decay * lam
                grad = back * before[8 * e : 8 * e + 8]
                rate_sum[e] = rate_sum[e] + grad * rate
                weighted[e] = weighted[e] + lam * inm
                b.ga[n, e] += grad * size[e]
                din = din + lam * push[e]
                dout = dout + dmix[e] * after[8 * e : 8 * e + 8]
                new.append(back)
            dins.append(din)
            douts.append(dout)
        for e in range(2):
            b.ys[e, at, :] = rate_sum[e] * LN2 + conv[e] * weighted[e]
            b.xc[e, at, :] = size[e] * weighted[e]
        return tuple(new), dins, douts

    def backward_step(i, carry):
        t = SLOT - 2 - 2 * i
        carry, din1, dout1 = backward_one(t + 1, carry)
        carry, din0, dout0 = backward_one(t, carry)
        for n in range(STATE):
            b.sall[t + 2, n] = jnp.concatenate([din0[n], din1[n]], axis=0).astype(BF16)
            b.sall[t + 3, n] = jnp.concatenate([dout0[n], dout1[n]], axis=0).astype(BF16)
        return carry

    carry = tuple(zero for _ in range(2 * STATE))
    carry = lax.fori_loop(0, SLOT // 4, backward_step, carry)
    bthree = reduce_third(3, btwo)
    carry = lax.fori_loop(SLOT // 4, SLOT // 2, backward_step, carry)
    reduce_end(3, bthree, bsum)
    for n in range(STATE):
        row = jnp.concatenate(
            [jnp.sum(b.ga[n, e] * b.rate[n, e], axis=0, keepdims=True) for e in range(2)], axis=1
        )
        b.sg[RANK + n : RANK + n + 1, :] = row * LN2

    bias_row = o + CONV + 1
    trow = lax.broadcasted_iota(jnp.int32, (256, 128), 0)
    tcol = lax.broadcasted_iota(jnp.int32, (256, 128), 1)
    maps = jnp.zeros((8 * SLOT, 128), F32)
    for k in range(2):
        for n in range(0, STATE, 2):
            left = b.sall[2:, n].reshape(SLOT // 2, 2, 16, 128)[:, k].reshape(8 * SLOT, 128)
            right = b.sall[2:, n + 1].reshape(SLOT // 2, 2, 16, 128)[:, k].reshape(8 * SLOT, 128)
            ones = jnp.where(tcol == RANK + k * STATE + n + trow // 128, 1.0, 0.0).astype(BF16)
            maps = maps + nn(jnp.concatenate([left, right], axis=1), ones)
    b.tm[...] = maps


    @pl.loop(0, 4)
    def _(q):
        for cc in range(2):
            j = 2 * q + cc
            rows = pl.ds(pl.multiple_of(j * SLOT, SLOT), SLOT)
            step_pre = nn(b.slow[rows, :], b.wst[...]) + sbias
            dstep = jnp.concatenate([b.ys[0, rows, :], b.ys[1, rows, :]], axis=1)
            dpre = dstep * jax.nn.sigmoid(step_pre)
            b.sg[bias_row : bias_row + 1, :] += jnp.sum(dpre, axis=0, keepdims=True)
            low = dpre.astype(BF16)
            b.dsl[j] = low
            b.pp[q, cc] = nt(low, b.wst[...]) + b.tm[pl.ds(j, SLOT, stride=8), :]

    ystate = [None, None]

    def pump_second(stage):
        if stage == 0:
            grad = tn(b.slow[...], b.dsl[...].reshape(8 * SLOT, cols))
            b.sg[0:RANK, :] = grad[:RANK]
        if stage == 1:
            ystate[0] = weight_sum(2, zgo)
        if stage == 2:
            ystate[1] = weight_sum(1, zgg)

    all_reduce(2, pump_second)

    tap_row = o

    @pl.loop(0, 4)
    def _(q):
        for cc, src in ((c, sets[2].own), (oc, sets[2].oth)):
            j = 2 * q + cc
            rows = pl.ds(pl.multiple_of(j * SLOT, SLOT), SLOT)
            dproj = src[q].astype(BF16)
            b.dpj[rows, :] = dproj
            dmix = jnp.concatenate([b.dm[0, rows, :], b.dm[1, rows, :]], axis=1)
            dconv = jnp.concatenate([b.xc[0, rows, :], b.xc[1, rows, :]], axis=1) + dmix * skip
            dconv = dconv + nt(dproj, wpl)
            cpre = jnp.broadcast_to(cbias, (SLOT, cols))
            for k in range(CONV):
                cpre = cpre + taps[k] * b.ip[j, 5 + k : 5 + k + SLOT, :]
            sig = jax.nn.sigmoid(cpre)
            dpre = dconv * (sig * (1.0 + cpre * (1.0 - sig)))
            b.dcp[0:SLOT, :] = dpre
            sums = [jnp.sum(dpre * b.ip[j, 5 + k : 5 + k + SLOT, :], axis=0, keepdims=True) for k in range(CONV)]
            sums.append(jnp.sum(dpre, axis=0, keepdims=True))
            b.sg[tap_row : tap_row + CONV + 1, :] += jnp.concatenate(sums, axis=0)
            dinner = taps[CONV - 1] * dpre
            for k in range(CONV - 1):
                dinner = dinner + taps[k] * b.dcp[CONV - 1 - k : CONV - 1 - k + SLOT, :]
            b.di[q, cc] = dinner.astype(BF16)

    zgi = weight_grad(0, b.di, b.nb, True, False)
    for i in range(8):
        b.vs[0, i : i + 1, :] = b.vv[:, i * 128 : i * 128 + 128]
    v1 = rcopy(b.vs.at[0], b.vl.at[0], core)

    gproj = tn(b.cl[...].reshape(8 * SLOT, cols), b.dpj[...])
    b.gps[...] = gproj.reshape(depth, hl, 128).astype(BF16)
    for i in range(depth):
        cut = b.sg[:, i * hl : (i + 1) * hl]
        b.sgs[i] = jnp.concatenate([cut, jnp.zeros((PACK, 128 - hl), F32)], axis=1).astype(BF16)
    zgs = [rcopy(b.sgs.at[q], b.sgl.at[k], dev) for k, (q, dev) in enumerate(zip(zpos, zpeers))]
    zgp = [rcopy(b.gps.at[q], b.gpl.at[k], dev) for k, (q, dev) in enumerate(zip(zpos, zpeers))]

    settle([bone, *btwo, *bthree])
    done = reduce_begin(
        3,
        lambda cc, chunk: nn(b.di[:, cc].reshape(4 * SLOT, cols), b.ws[0, :, chunk])
        + nn(b.dg[:, cc].reshape(4 * SLOT, cols), b.ws[1, :, chunk]),
    )
    dtwo = reduce_second(3, done)
    v1.wait_recv()
    b.vs[1] = b.vs[0] + b.vl[0]
    v2 = rcopy(b.vs.at[1], b.vl.at[1], xpeer)
    dthree = reduce_third(3, dtwo)
    v2.wait_recv()
    b.vs[2] = b.vs[1] + b.vl[1]
    v3 = rcopy(b.vs.at[2], b.vl.at[2], ypeer)
    for w in (2, 1):
        ystate[2 - w].wait_recv()
        gout[w, 1 - y] = b.gyl[w].astype(F32)
    yin = weight_sum(0, zgi)

    total = b.sgs[f].astype(F32)
    for k, cp in enumerate(zgs):
        cp.wait_recv()
        total = total + b.sgl[k].astype(F32)
    sout[y] = total
    b.sgt[...] = total.astype(BF16)
    ys1 = rcopy(b.sgt, b.sgy, ypeer)
    total = b.gps[f].astype(F32)
    for k, cp in enumerate(zgp):
        cp.wait_recv()
        total = total + b.gpl[k].astype(F32)
    pout[y] = total
    b.gpt[...] = total.astype(BF16)
    ys2 = rcopy(b.gpt, b.gpy, ypeer)
    v3.wait_recv()
    b.vs[3] = b.vs[2] + b.vl[2]
    v4 = [rcopy(b.vs.at[3], b.vz.at[k], dev) for k, dev in enumerate(zpeers)]
    reduce_end(3, dthree, dsc)
    total = b.vs[3]
    for k, cp in enumerate(v4):
        cp.wait_recv()
        total = total + b.vz[k]
    vout[...] = total
    yin.wait_recv()
    gout[0, 1 - y] = b.gyl[0].astype(F32)
    ys1.wait_recv()
    sout[1 - y] = b.sgy[...].astype(F32)
    ys2.wait_recv()
    pout[1 - y] = b.gpy[...].astype(F32)
    for cp in started:
        cp.wait_send()


def last_kernel(hl, piece, tok, cot, lens, bsum, dsc, gout, sout, pout, vout, *outs):
    (out, dtok, ggain, ginner, ggate, gconv, gcb, gproj, gstep, gsb, glog, gskip, gwout) = outs
    s = lax.axis_index("shard")
    t32 = tok[...].astype(F32)
    rowid = lax.broadcasted_iota(jnp.int32, (SLOT, 1), 0)
    out[...] = (t32 + jnp.where(rowid < lens[0], bsum[...], 0.0)).astype(BF16)
    inv = lax.rsqrt(jnp.mean(t32 * t32, axis=1, keepdims=True) + EPS)
    ds = dsc[...]
    mean = jnp.mean(ds * t32, axis=1, keepdims=True)
    dtok[...] = cot[...].astype(F32) + inv * ds - t32 * (inv * inv * inv * mean)
    width = tok.shape[1]
    el = 2 * hl
    ginner[...] = gout[0].reshape(el, width).T
    ggate[...] = gout[1].reshape(el, width).T
    gwout[...] = gout[2].reshape(el, width)
    gproj[...] = pout[...].reshape(el, 128)[:, : RANK + 2 * STATE]
    both = jnp.concatenate([sout[0][:, :hl], sout[1][:, :hl]], axis=1)
    o = RANK + STATE
    gstep[...] = both[:RANK]
    glog[...] = both[RANK:o]
    gconv[...] = both[o : o + CONV]
    gcb[...] = both[o + CONV : o + CONV + 1]
    gsb[...] = both[o + CONV + 1 : o + CONV + 2]
    gskip[...] = both[o + CONV + 2 : o + CONV + 3]
    per = 128 // piece
    vec = vout[...]
    rows = lax.broadcasted_iota(jnp.int32, (8, 128), 0)
    row = jnp.sum(jnp.where(rows == s // per, vec, 0.0), axis=0, keepdims=True)
    pick = jnp.zeros((1, piece), F32)
    for i in range(per):
        pick = jnp.where(lax.rem(s, per) == i, row[:, i * piece : (i + 1) * piece], pick)
    ggain[...] = pick


def make_local(replicas, shards):
    depth = shards // 4

    def local(
        tokens, norm_gain, w_inner, w_gate, conv_weight, conv_bias, w_proj, w_step, step_bias, a_log, skip_gain,
        w_out, cotangent, lengths,
    ):
        width = tokens.shape[1]
        el = w_inner.shape[1]
        hl = el // 2
        piece = norm_gain.shape[0]
        pack = jnp.concatenate(
            [w_step, a_log, conv_weight, conv_bias[None], step_bias[None], skip_gain[None]], axis=0
        )
        pack = jnp.pad(pack, ((0, PACK - pack.shape[0]), (0, 128 - el)))
        gain = jnp.pad(
            jnp.broadcast_to(norm_gain.astype(F32)[None], (8, piece)), ((0, 0), (0, 128 - piece))
        )
        spec = buffers(depth, hl, width, shards, piece)
        nsem = 96 + 16 * depth
        vm = pl.BlockSpec(memory_space=pltpu.VMEM)
        sm = pl.BlockSpec(memory_space=pltpu.SMEM)
        sds = jax.ShapeDtypeStruct
        mid = pl.pallas_call(
            functools.partial(main_kernel, [tuple(group) for group in spec], depth, hl, piece, nsem),
            out_shape=(
                sds((SLOT, width), F32),
                sds((SLOT, width), F32),
                sds((3, 2, hl, width), F32),
                sds((2, PACK, 128), F32),
                sds((2, hl, 128), F32),
                sds((8, 128), F32),
            ),
            in_specs=[vm] * 8 + [sm],
            out_specs=(vm,) * 6,
            scratch_shapes=[pltpu.VMEM(shape, kind) for group in spec for shape, kind in group.values()]
            + [pltpu.SemaphoreType.DMA((nsem,)), pltpu.SemaphoreType.DMA((nsem,))],
            compiler_params=pltpu.CompilerParams(
                collective_id=0, has_side_effects=True, vmem_limit_bytes=61 << 20
            ),
            name="layer",
        )(tokens, cotangent, w_inner, w_gate, w_out, w_proj, pack, gain, lengths)
        bsum, dsc, gout, sout, pout, vout = mid
        if replicas > 2:
            groups = [[r for r in range(replicas) if r % 2 == k] for k in range(2)]
            gout, sout, pout, vout = (
                lax.psum(v, "replica", axis_index_groups=groups) for v in (gout, sout, pout, vout)
            )
        outs = pl.pallas_call(
            functools.partial(last_kernel, hl, piece),
            out_shape=(
                sds((SLOT, width), BF16),
                sds((SLOT, width), F32),
                sds((1, piece), F32),
                sds((width, el), F32),
                sds((width, el), F32),
                sds((CONV, el), F32),
                sds((1, el), F32),
                sds((el, RANK + 2 * STATE), F32),
                sds((RANK, el), F32),
                sds((1, el), F32),
                sds((STATE, el), F32),
                sds((1, el), F32),
                sds((el, width), F32),
            ),
            in_specs=[vm, vm, sm] + [vm] * 6,
            out_specs=(vm,) * 13,
            name="results",
        )(tokens, cotangent, lengths, bsum, dsc, gout, sout, pout, vout)
        return tuple(v.reshape(-1) if v.shape[0] == 1 else v for v in outs)

    return local


def solution(mesh):
    return jax.shard_map(
        make_local(mesh.shape["replica"], mesh.shape["shard"]),
        mesh=mesh,
        in_specs=(
            P(("replica", "shard"), None),
            P("shard"),
            P(None, "shard"),
            P(None, "shard"),
            P(None, "shard"),
            P("shard"),
            P("shard", None),
            P(None, "shard"),
            P("shard"),
            P(None, "shard"),
            P("shard"),
            P("shard", None),
            P(("replica", "shard"), None),
            P(("replica", "shard")),
        ),
        out_specs=(
            P(("replica", "shard"), None),
            P(("replica", "shard"), None),
            P("shard"),
            P(None, "shard"),
            P(None, "shard"),
            P(None, "shard"),
            P("shard"),
            P("shard", None),
            P(None, "shard"),
            P("shard"),
            P(None, "shard"),
            P("shard"),
            P("shard", None),
        ),
        check_vma=False,
    )
```

time: 1710 us -> 131 us (0.08); the launches traced: 1690 us -> 131 us
  local copies, waits for them, and re-layouts: 580 us -> 6.36 us
  other arithmetic: 390 us -> 0.66 us
  waiting for transfers between devices: 376 us -> 0 us
  blocking collectives: 236 us -> 0 us
  Pallas kernels: 0 us -> 123 us
  matrix products: 57.8 us -> 0 us
  loops' own time: 32.6 us -> 0 us
    pad x60 -> x2, local copies, waits for them, and re-layouts: 462 us -> 1.21 us  [the longest x1 0.61 us: local(): pack = jnp.pad(pack, ((0, PACK - pack.shape[0]), (0, 128 - el)))]
    unnamed x17 -> x0, waiting for transfers between devices: 280 us -> none
    add x66 -> x0, other arithmetic: 175 us -> none  [the longest x30 89.1 us: combine(): return (earlier[0] * later[0], later[0] * earlier[1] + later[1])]
    all_gather x7 -> x0, blocking collectives: 133 us -> none  [the longest x1 21 us: local(): lax.all_gather(w_proj, 'shard', axis=0, tiled=True)]
    pallas_call x0 -> x2, Pallas kernels: none -> 123 us  [the longest x1 119 us: local(): pl.pallas_call(functools.partial(main_kernel, [tuple(group) for group in...]
    mul x28 -> x0, other arithmetic: 96.1 us -> none  [the longest x24 86.2 us: combine(): return (earlier[0] * later[0], later[0] * earlier[1] + later[1])]
    unnamed x2 -> x0, blocking collectives: 94.9 us -> none
    reduce_scatter x1 -> x0, waiting for transfers between devices: 73.4 us -> none  [local(): lax.psum_scatter(gradients[10].astype(jnp.bfloat16), 'shard', scatter_dim...]
  transfers between devices with their start and end apart: 11 -> 0, of which waited for: 7 -> 0; matrix products, arithmetic and copies ran while one was open for 4% -> 0% of each run, Pallas kernels for 0% -> 0%
where the time goes in v1:
time: 131 us
  Pallas kernels  123 us (94%)
  local copies, waits for them, and re-layouts  6.36 us (5%)
  between operations  1.31 us (1%)
    pallas_call x1, Pallas kernels, local(): pl.pallas_call(functools.partial(main_kernel, [tuple(group) for group in...  119 us
    pallas_call x1, Pallas kernels, local(): pl.pallas_call(functools.partial(last_kernel, hl, piece), out_shape=(sds(...  3.72 us
    unnamed x2, local copies, waits for them, and re-layouts  3 us

profile of v1, /device:TPU:0, one launch (start us, length us, event | category | flops | bytes accessed | tf_op | source)
XLA Modules:
  0.0 131.0 jit_solution(7907970768528028841)
XLA Ops:
  1.3 0.7 pad_convert_fusion
  1.9 0.6 pad.15.refs_7_
  2.5 2.1 %concatenate.3 = bf16[87,128]{1,0:T(8,128)(2,1)S(1)} concatenate(bf16[64,128]{1,0:T(8,128)(2,1)} %param.21, bf16[16,128]{1,0:T(8,128)(2,1)} %param.23, bf16[4,128]{1,0:T(4,128)(2,1)} %param.18, bf16[1,128]{1,0:T(2,128)(2,1)} %bitcast.7, bf16[1,128]{1,0:T(2,128)(2,1)} %bitcast.8, bf16[1,128]{1,0:T(2,128)(2,1)} %bitcast.9), dimensions={0} | concatenate | bytes 44544 | tf_op jit(solution)/shard_map/concatenate | solution.py:749
  4.7 0.6 pad.12.refs_6_
  5.3 1.5 %copy.27.refs_5_ = bf16[128,96]{1,0:T(8,128)(2,1)} copy(bf16[128,96]{0,1:T(8,128)(2,1)} %param.20) | data formatting | bytes 49152 | tf_op args[6]
  6.8 119.0 %layer.1 = (f32[128,1024]{1,0:T(8,128)}, f32[128,1024]{1,0:T(8,128)}, f32[3,2,64,1024]{3,2,1,0:T(8,128)}, f32[2,96,128]{2,1,0:T(8,128)}, f32[2,64,128]{2,1,0:T(8,128)}, /*index=5*/f32[8,128]{1,0:T(8,128)}) custom-call(bf16[128,1024]{1,0:T(8,128)(2,1)} %tok.1, bf16[128,1024]{1,0:T(8,128)(2,1)} %cot.1, bf16[1024,128]{1,0:T(8,128)(2,1)} %refs_2_.1, ...), custom_call_target="tpu_custom_call" | custom-call | tf_op jit(solution)/shard_map/layer/pallas_call | solution.py:761
  125.7 3.7 %results.1 = (bf16[128,1024]{1,0:T(8,128)(2,1)}, f32[128,1024]{1,0:T(8,128)}, f32[1,64]{1,0:T(1,128)}, f32[1024,128]{1,0:T(8,128)}, f32[1024,128]{1,0:T(8,128)},...) custom-call(bf16[128,1024]{1,0:T(8,128)(2,1)} %tok.1, ...), custom_call_target="tpu_custom_call" | custom-call | tf_op jit(solution)/shard_map/results/pallas_call | solution.py:786
  129.5 1.6 %copy.28 = f32[128,96]{0,1:T(8,128)} copy(f32[128,96]{1,0:T(8,128)} %get-tuple-element.58) | data formatting | bytes 98304

commit v2 on v1

v2 whole, which is shorter than its diff:
```python
import functools
import math
from types import SimpleNamespace

import jax
import jax.numpy as jnp
from jax import lax
from jax.experimental import pallas as pl
from jax.experimental.pallas import tpu as pltpu
from jax.sharding import PartitionSpec as P

RANK = 64
STATE = 16
CONV = 4
SLOT = 128
EPS = 1e-05
LN2 = math.log(2.0)
PROJ = RANK + 2 * STATE
PACK = 192
STEP_ROW = PROJ
LOG_ROW = STEP_ROW + RANK
TAP_ROW = LOG_ROW + STATE
CONV_ROW = TAP_ROW + CONV
BIAS_ROW = CONV_ROW + 1
SKIP_ROW = BIAS_ROW + 1
GAIN_ROW = SKIP_ROW + 1
MESH = pl.DeviceIdType.MESH
F32 = jnp.float32
BF16 = jnp.bfloat16


def sigmoid(value):
    return 0.5 * jnp.tanh(0.5 * value) + 0.5


def nt(left, right):
    return lax.dot_general(left, right, (((1,), (1,)), ((), ())), preferred_element_type=F32)


def nn(left, right):
    return lax.dot_general(left, right, (((1,), (0,)), ((), ())), preferred_element_type=F32)


def tn(left, right):
    return lax.dot_general(left, right, (((0,), (0,)), ((), ())), preferred_element_type=F32)


def buffers(depth, hl, width, shards, piece):
    cols = depth * hl
    rows = 8 * SLOT
    reduce_small = dict(
        s1=((4, SLOT, 128), BF16),
        l1=((4, SLOT, 128), BF16),
        s2=((4, SLOT, 128), BF16),
        l2=((4, SLOT, 128), BF16),
        s3=((4, SLOT, 128), BF16),
        l3=((4, SLOT, 128), BF16),
        own=((4, SLOT, 128), F32),
        oth=((4, SLOT, 128), F32),
    )
    reduce_large = dict(
        s1=((4, SLOT, width), BF16),
        l1=((4, SLOT, width), BF16),
        sx=((2, SLOT // 2, width), BF16),
        sy=((2, SLOT // 2, width), BF16),
        lx=((2, SLOT // 2, width), BF16),
        ly=((2, SLOT // 2, width), BF16),
        tx=((SLOT // 2, width), BF16),
        ty=((SLOT // 2, width), BF16),
        mx=((SLOT // 2, width), BF16),
        my=((SLOT // 2, width), BF16),
    )
    shapes = dict(
        wt=((3, depth, hl, width), BF16),
        ws=((2, cols, width), BF16),
        pka=((depth, PACK // 2, 128), BF16),
        wpt=((128, cols), BF16),
        gb=((2, 2, 8, cols), F32),
        t1=((rows, cols), F32),
        t2=((rows, cols), F32),
        gl=((1, width), F32),
        nb=((4, 2, SLOT, width), BF16),
        db=((4, 2, SLOT, width), BF16),
        pkl=((PACK, cols), F32),
        wst=((128, cols), BF16),
        rate=((STATE, 2, 8, 128), F32),
        ip=((8, SLOT + 8, cols), F32),
        dcp=((SLOT + 8, cols), F32),
        tm=((rows, 128), F32),
        sel=((256, 2 * STATE * 128), BF16),
        bc=((SLOT, 2 * STATE, 8, 128), F32),
        sall=((SLOT // 2 + 1, STATE, 2, 16, 128), BF16),
        cl=((8, SLOT, cols), BF16),
        xc=((2, rows, 128), F32),
        pp=((4, 2, SLOT, 128), F32),
        slow=((rows, 128), BF16),
        dpj=((rows, 128), BF16),
        dt=((2, rows, 128), F32),
        ys=((2, rows, 128), F32),
        dm=((2, rows, 128), F32),
        ga=((STATE, 2, 8, 128), F32),
        go=((4, 2, SLOT, cols), BF16),
        dg=((4, 2, SLOT, cols), BF16),
        di=((4, 2, SLOT, cols), BF16),
        dsl=((8, SLOT, cols), BF16),
        gws=((3, depth, hl, width), BF16),
        gwl=((3, depth - 1, hl, width), BF16),
        gwx=((3, hl, width), BF16),
        sg=((PACK, cols), F32),
        sgs=((depth, PACK // 2, 128), BF16),
        sgl=((depth - 1, PACK // 2, 128), BF16),
        sgx=((PACK // 2, 128), BF16),
        vv=((1, width), F32),
        sum=((4, SLOT, width), F32),
        vs=((4, 8, 128), F32),
        vl=((3, 8, 128), F32),
        vz=((depth, 8, 128), F32),
    )
    return [shapes, reduce_small, reduce_small, reduce_large]


def main_kernel(names, depth, hl, piece, nsem, *refs):
    (tok, cot, win, wg, wo, wproj, wstep, alog, convw, convb, stepb, skipg, gain, lens) = refs[:14]
    (bsum, dsc, gout, sout, vout) = refs[14:19]
    send_sems, recv_sems = refs[-2:]
    sets, at = [], 19
    for group in names:
        sets.append(SimpleNamespace(**dict(zip(group, refs[at:]))))
        at += len(group)
    b = sets[0]
    width = tok.shape[1]
    cols = depth * hl
    el = 2 * hl
    count = 8 * SLOT
    half = SLOT // 2

    r = lax.axis_index("replica")
    s = lax.axis_index("shard")
    y = lax.rem(r, 2)
    f = s // 4
    x = lax.rem(s // 2, 2)
    c = lax.rem(s, 2)
    core = (r, s + 1 - 2 * c)
    xpeer = (r, s + 2 - 4 * x)
    ypeer = (r + 1 - 2 * y, s)
    zpos = [lax.rem(f + k, depth) for k in range(1, depth)]
    zpeers = [(r, s + 4 * (q - f)) for q in zpos]
    q0 = y * 2 + x
    qx = y * 2 + 1 - x
    qy = (1 - y) * 2 + x
    qd = (1 - y) * 2 + 1 - x
    oc = 1 - c
    top, low = slice(0, half), slice(half, SLOT)

    counter = [0]
    started = []
    line = depth == 4
    ends = (f == 0) | (f == 3)
    inner = (f == 1) | (f == 2)

    def ticket():
        counter[0] += 1
        assert counter[0] <= nsem
        return counter[0] - 1

    def remote(src, dst, dev, send, recv):
        return pltpu.make_async_remote_copy(
            src_ref=src,
            dst_ref=dst,
            send_sem=send_sems.at[send],
            recv_sem=recv_sems.at[recv],
            device_id=dev,
            device_id_type=MESH,
        )

    def rcopy(src, dst, dev):
        i = ticket()
        cp = remote(src, dst, dev, i, i)
        cp.start()
        started.append(cp)
        return cp

    def same(ref, dev):
        return rcopy(ref, ref, dev)

    def settle(cps):
        for cp in cps:
            cp.wait_send()
            started[:] = [other for other in started if other is not cp]

    def arrive(cps):
        for cp in cps:
            cp.wait_recv()

    def only(when, cp):
        @pl.when(when)
        def _():
            cp.start()

        def wait_send():
            @pl.when(when)
            def _():
                cp.wait_send()

        started.append(SimpleNamespace(wait_send=wait_send))

    def far(k):
        return ((f == 0) & (k == 3)) | ((f == 3) & (k == 1))

    def far_from(k):
        return ((f == 0) & (k == 1)) | ((f == 3) & (k == 3))

    def z_gather(piece):
        ids = [ticket() for _ in range(depth)]
        cps = {}
        for k in sorted(range(1, depth), key=lambda k: k != 2):
            cps[k] = remote(piece(f), piece(f), zpeers[k - 1], ids[k], ids[k])
            if line and k != 2:
                only(jnp.logical_not(far(k)), cps[k])
            else:
                cps[k].start()
                started.append(cps[k])
        return SimpleNamespace(piece=piece, ids=ids, cps=cps)

    def z_relay(st):
        if line:
            st.cps[2].wait_recv()
            q = 3 * (2 - jnp.where(inner, f, 1))
            near = jnp.where(inner, 2 * f - 1, 1)
            only(inner, remote(st.piece(q), st.piece(q), (r, s + 4 * (3 - q - f)), st.ids[0], st.ids[1] + near - 1))

    def z_arrive(st):
        for k in range(1, depth):
            if not (line and k == 2):
                st.cps[k].wait_recv()

    def z_scatter(send, land, extra):
        ids = [ticket() for _ in range(depth)]
        cps = {k: remote(send(zpos[k - 1]), land(k - 1), zpeers[k - 1], ids[k], ids[k]) for k in range(1, depth)}
        st = SimpleNamespace(send=send, land=land, extra=extra, cps=cps)
        if not line:
            for cp in cps.values():
                cp.start()
                started.append(cp)
            return st
        st.cross = remote(send(3 - f), extra, (r, s + 4 - 8 * (f // 3)), ids[0], ids[0])
        only(ends, st.cross)
        return st

    def z_direct(st):
        if line:
            only(ends, st.cps[2])
            for k in (1, 3):
                only(jnp.logical_not(far(k)), st.cps[k])
        return st

    def z_absorb(st):
        if line:

            @pl.when(inner)
            def _():
                st.cross.wait_recv()
                target = st.send(zpos[1])
                target[...] = (target[...].astype(F32) + st.extra[...].astype(F32)).astype(BF16)

            only(inner, st.cps[2])

    def z_sum(st, own):
        total = own
        for k in range(1, depth):
            if line and k != 2:

                @pl.when(jnp.logical_not(far_from(k)))
                def _():
                    st.cps[k].wait_recv()

            else:
                st.cps[k].wait_recv()
        for k in range(1, depth):
            value = st.land(k - 1)[...].astype(F32)
            total = total + (jnp.where(far_from(k), 0.0, value) if line and k != 2 else value)
        return total

    barrier = pltpu.get_barrier_semaphore()
    reach = [core, xpeer, ypeer]
    for dev in reach:
        pl.semaphore_signal(barrier, inc=1, device_id=dev, device_id_type=MESH)
    for k in range(1, depth):

        def hello():
            pl.semaphore_signal(barrier, inc=1, device_id=zpeers[k - 1], device_id_type=MESH)

        if line and k != 2:
            pl.when(jnp.logical_not(far(k)))(hello)
        else:
            hello()

    def lanes(value, n):
        value = value.astype(F32)
        if value.shape[1] == n:
            return value
        return jnp.concatenate([value, jnp.zeros((value.shape[0], n - value.shape[1]), F32)], axis=1)

    def folded(value, n):
        both = jnp.concatenate([value[: PACK // 2], value[PACK // 2 :]], axis=1)
        return lanes(both, 128).astype(BF16)

    def unfolded(value, n):
        return jnp.concatenate([value[:, :n], value[:, n : 2 * n]], axis=0)

    rows = [wproj[...], wstep[...], alog[...], convw[...]]
    rows += [v[...].reshape(1, el) for v in (convb, stepb, skipg)]
    rows = [v.astype(F32) for v in rows]
    rows.append(jnp.zeros((PACK - GAIN_ROW, el), F32))
    pack = jnp.concatenate(rows, axis=0)
    mine = jnp.where(y == 0, pack[:, :hl], pack[:, hl:])
    own_gain = gain[...].reshape(1, piece).astype(F32)
    rowid = lax.broadcasted_iota(jnp.int32, (PACK, 1), 0)
    b.pka[f] = folded(jnp.where(rowid == GAIN_ROW, own_gain, mine), hl)
    wint = win[...].T
    b.wt[0, f] = jnp.where(y == 0, wint[:hl], wint[hl:])
    t32 = tok[...].astype(F32)
    inv = lax.rsqrt(jnp.mean(t32 * t32, axis=1, keepdims=True) + EPS)
    b.nb[q0, c] = (t32 * inv).astype(BF16)

    if line:
        for w in range(3):
            for k in (1, 3):

                @pl.when(far_from(k))
                def _():
                    b.gwl[w, k - 1] = jnp.zeros((hl, width), BF16)

        for k in (1, 3):

            @pl.when(far_from(k))
            def _():
                b.sgl[k - 1] = jnp.zeros((PACK // 2, 128), BF16)

        pl.semaphore_wait(barrier, jnp.where(ends, 5, 6))
    else:
        pl.semaphore_wait(barrier, 2 + depth)

    def plane_start(buf):
        upper, lower = buf.at[q0, c, pl.ds(0, half)], buf.at[q0, c, pl.ds(half, half)]
        ax = same(upper, xpeer)
        by = same(lower, ypeer)
        bx = same(lower, xpeer)
        ay = same(upper, ypeer)
        oo = same(buf.at[q0, c], core)
        return ax, by, bx, ay, oo

    def plane_forward(buf, cps):
        ax, by, bx, ay, oo = cps
        ax.wait_recv()
        fa = same(buf.at[qx, c, pl.ds(0, half)], ypeer)
        by.wait_recv()
        fb = same(buf.at[qy, c, pl.ds(half, half)], xpeer)
        return bx, ay, oo, fa, fb

    def plane_core(buf, cps):
        bx, ay, oo, fa, fb = cps
        bx.wait_recv()
        ox = same(buf.at[qx, c], core)
        ay.wait_recv()
        oy = same(buf.at[qy, c], core)
        return oo, ox, oy, fa, fb

    def plane_last(buf, cps):
        oo, ox, oy, fa, fb = cps
        arrive([fa, fb])
        return oo, ox, oy, same(buf.at[qd, c], core)

    zsmall = z_gather(lambda q: b.pka.at[q])
    zin = z_gather(lambda q: b.wt.at[0, q])
    nstate = plane_start(b.nb)

    wgt = wg[...].T
    b.wt[1, f] = jnp.where(y == 0, wgt[:hl], wgt[hl:])
    b.wt[2, f] = wo[pl.ds(y * hl, hl), :]
    rowid = lax.broadcasted_iota(jnp.int32, (SLOT, 1), 0)
    b.db[q0, c] = jnp.where(rowid < lens[0], cot[...].astype(F32), 0.0).astype(BF16)
    z_relay(zsmall)
    nstate = plane_forward(b.nb, nstate)
    z_relay(zin)
    zgate = z_gather(lambda q: b.wt.at[1, q])
    zout = z_gather(lambda q: b.wt.at[2, q])
    z_arrive(zsmall)
    locs = [unfolded(b.pka[i].astype(F32), hl) for i in range(depth)]
    pkl = jnp.concatenate(locs, axis=1)
    b.pkl[...] = pkl
    b.gb[c, x] = jnp.broadcast_to(pkl[GAIN_ROW : GAIN_ROW + 1], (8, cols))
    gx = same(b.gb.at[c, x], xpeer)
    dstate = plane_start(b.db)
    b.wst[...] = jnp.concatenate(
        [pkl[STEP_ROW:LOG_ROW], jnp.zeros((128 - RANK, cols), F32)], axis=0
    ).astype(BF16)
    b.wpt[...] = jnp.concatenate([pkl[:PROJ], jnp.zeros((128 - PROJ, cols), F32)], axis=0).astype(BF16)
    for n in range(STATE):
        row = -jnp.exp(pkl[LOG_ROW + n : LOG_ROW + n + 1]) * (1.0 / LN2)
        for et in range(2):
            b.rate[n, et] = jnp.broadcast_to(row[:, et * 128 : et * 128 + 128], (8, 128))
    nstate = plane_core(b.nb, nstate)
    b.ip[:, 0:8, :] = jnp.zeros((8, 8, cols), F32)
    b.dcp[SLOT : SLOT + 8, :] = jnp.zeros((8, cols), F32)
    b.ga[...] = jnp.zeros((STATE, 2, 8, 128), F32)
    b.sall[0] = jnp.zeros((STATE, 2, 16, 128), BF16)
    b.sg[...] = jnp.zeros((PACK, cols), F32)
    source = lax.broadcasted_iota(jnp.int32, (256, 2 * STATE * 128), 0)
    target = lax.broadcasted_iota(jnp.int32, (256, 2 * STATE * 128), 1)
    b.sel[...] = jnp.where(lax.rem(source, 128) == RANK + target // 128, 1.0, 0.0).astype(BF16)
    gx.wait_recv()
    gc = same(b.gb.at[c], core)
    gc.wait_recv()
    pieces = []
    for i in range(depth):
        for j in range(2):
            for k in range(2):
                pieces.append(b.gb[k, j, 0:1, i * piece : (i + 1) * piece])
    b.gl[...] = jnp.concatenate(pieces, axis=1)

    z_arrive(zin)
    z_relay(zgate)

    def scaled(w):
        full = b.wt[w].reshape(cols, width).astype(F32)
        b.ws[w] = (full * b.gl[...]).astype(BF16)

    scaled(0)
    arrive(plane_last(b.nb, nstate))

    def row_of(i):
        return b.pkl[i : i + 1, :]

    taps = [row_of(TAP_ROW + k) for k in range(CONV)]
    cbias = row_of(CONV_ROW)
    sbias = row_of(BIAS_ROW)
    skip = row_of(SKIP_ROW)

    def slot_rows(j):
        return pl.ds(pl.multiple_of(j * SLOT, SLOT), SLOT)

    def pair(ref, at):
        return jnp.concatenate([ref[0, at, :], ref[1, at, :]], axis=1)

    def unpair(ref, at, value):
        ref[0, at, :] = value[:, :128]
        ref[1, at, :] = value[:, 128:]

    def convolved(j):
        acc = jnp.broadcast_to(cbias, (SLOT, cols))
        for k in range(CONV):
            acc = acc + taps[k] * b.ip[j, 5 + k : 5 + k + SLOT, :]
        return acc

    b.ip[:, 8 : 8 + SLOT, :] = nt(b.nb[...].reshape(count, width), b.ws[0]).reshape(8, SLOT, cols)

    @pl.loop(0, 8)
    def _(j):
        acc = convolved(j)
        out = acc * sigmoid(acc)
        unpair(b.xc, slot_rows(j), out)
        b.cl[j] = out.astype(BF16)

    b.pp[...] = nt(b.cl[...].reshape(count, cols), b.wpt[...]).reshape(4, 2, SLOT, 128)

    def all_reduce(which, between):
        g = sets[which]
        g.s1[...] = b.pp[:, oc].astype(BF16)
        one = rcopy(g.s1, g.l1, core)
        between(0)
        one.wait_recv()
        total = b.pp[:, c] + g.l1[...].astype(F32)
        g.s2[...] = total.astype(BF16)
        two = [
            rcopy(g.s2.at[pl.ds(0, 2)], g.l2.at[pl.ds(0, 2)], xpeer),
            rcopy(g.s2.at[pl.ds(2, 2)], g.l2.at[pl.ds(2, 2)], ypeer),
        ]
        g.own[...] = total
        between(1)
        arrive(two)
        total = g.own[...] + g.l2[...].astype(F32)
        g.s3[...] = total.astype(BF16)
        three = [
            rcopy(g.s3.at[pl.ds(0, 2)], g.l3.at[pl.ds(0, 2)], ypeer),
            rcopy(g.s3.at[pl.ds(2, 2)], g.l3.at[pl.ds(2, 2)], xpeer),
        ]
        g.own[...] = total
        between(2)
        arrive(three)
        g.own[...] = g.own[...] + g.l3[...].astype(F32)
        four = rcopy(g.own, g.oth, core)
        between(3)
        four.wait_recv()

    dhold = [dstate]

    def pump_first(stage):
        if stage == 1:
            z_relay(zout)
        if stage == 2:
            dhold[0] = plane_forward(b.db, dhold[0])
        if stage == 3:
            dhold[0] = plane_core(b.db, dhold[0])

    all_reduce(1, pump_first)

    @pl.loop(0, 4)
    def _(q):
        for cc, src in ((c, sets[1].own), (oc, sets[1].oth)):
            j = 2 * q + cc
            proj = src[q]
            b.tm[pl.ds(j, SLOT, stride=8), :] = proj
            b.slow[slot_rows(j), :] = proj.astype(BF16)

    b.t1[...] = nn(b.slow[...], b.wst[...])

    @pl.loop(0, 8)
    def _(j):
        at = slot_rows(j)
        pre = b.t1[at, :] + sbias
        unpair(b.dt, at, jnp.maximum(pre, 0.0) + jnp.log1p(jnp.exp(-jnp.abs(pre))))

    tm = b.tm[...]
    high = tm.astype(BF16)
    spread = jnp.concatenate([high, (tm - high.astype(F32)).astype(BF16)], axis=1)
    both = nn(spread, b.sel[...])
    for i in range(2 * STATE):
        b.bc[:, i] = both[:, i * 128 : i * 128 + 128].reshape(SLOT, 8, 128)

    dstate = plane_last(b.db, dhold[0])
    zero = jnp.zeros((8, 128), F32)

    def forward_pair(k, carry):
        ats = [pl.ds(2 * k + i, 8, stride=SLOT) for i in range(2)]
        size = [[b.dt[e, at, :] for e in range(2)] for at in ats]
        push = [[size[i][e] * b.xc[e, ats[i], :] for e in range(2)] for i in range(2)]
        out = [[zero, zero], [zero, zero]]
        new = []
        for n in range(STATE):
            inm = [b.bc[2 * k + i, n] for i in range(2)]
            outm = [b.bc[2 * k + i, STATE + n] for i in range(2)]
            for e in range(2):
                rate = b.rate[n, e]
                state = carry[2 * n + e]
                kept = []
                for i in range(2):
                    state = jnp.exp2(size[i][e] * rate) * state + push[i][e] * inm[i]
                    out[i][e] = out[i][e] + outm[i] * state
                    kept.append(state)
                b.sall[k + 1, n, e] = jnp.concatenate(kept, axis=0).astype(BF16)
                new.append(state)
        for i in range(2):
            for e in range(2):
                b.ys[e, ats[i], :] = out[i][e]
        return tuple(new)

    lax.fori_loop(0, SLOT // 2, forward_pair, tuple(zero for _ in range(2 * STATE)))

    arrive(dstate)
    z_arrive(zgate)
    scaled(1)
    b.t1[...] = nt(b.nb[...].reshape(count, width), b.ws[1])
    z_arrive(zout)
    b.t2[...] = nt(b.db[...].reshape(count, width), b.wt[2].reshape(cols, width))

    @pl.loop(0, 4)
    def _(q):
        for cc in range(2):
            at = slot_rows(2 * q + cc)
            gpre = b.t1[at, :]
            dgat = b.t2[at, :]
            conv = pair(b.xc, at)
            mixed = pair(b.ys, at) + skip * conv
            sig = sigmoid(gpre)
            act = gpre * sig
            b.go[q, cc] = (mixed * act).astype(BF16)
            dmix = dgat * act
            unpair(b.dm, at, dmix)
            slope = sig * (1.0 + gpre * (1.0 - sig))
            b.dg[q, cc] = (dgat * mixed * slope).astype(BF16)
            b.sg[SKIP_ROW : SKIP_ROW + 1, :] += jnp.sum(dmix * conv, axis=0, keepdims=True)

    def reduce_begin(dots):
        g = sets[3]
        g.s1[qd] = dots(lambda ref: ref[qd, oc]).astype(BF16)
        cores = [rcopy(g.s1.at[qd], g.l1.at[qd], core)]
        others = (qx, qy, q0)
        rest = dots(lambda ref: jnp.concatenate([ref[q, oc] for q in others], axis=0)).astype(BF16)
        for k, q in enumerate(others):
            g.s1[q] = rest[k * SLOT : (k + 1) * SLOT]
            cores.append(rcopy(g.s1.at[q], g.l1.at[q], core))
        b.sum[...] = dots(lambda ref: ref[:, c].reshape(4 * SLOT, cols)).reshape(4, SLOT, width)
        return cores

    def reduce_second(cores):
        g = sets[3]

        def chip(q, rows):
            return (b.sum[q, rows, :] + g.l1[q, rows, :].astype(F32)).astype(BF16)

        cores[0].wait_recv()
        g.sx[1] = chip(qd, top)
        x1 = rcopy(g.sx.at[1], g.lx.at[1], xpeer)
        g.sy[1] = chip(qd, low)
        y1 = rcopy(g.sy.at[1], g.ly.at[1], ypeer)
        cores[1].wait_recv()
        g.sx[0] = chip(qx, top)
        x0 = rcopy(g.sx.at[0], g.lx.at[0], xpeer)
        cores[2].wait_recv()
        g.sy[0] = chip(qy, low)
        y0 = rcopy(g.sy.at[0], g.ly.at[0], ypeer)
        return x1, y1, x0, y0

    def reduce_third(cps):
        g = sets[3]
        x1, y1, x0, y0 = cps
        x1.wait_recv()
        g.ty[...] = (b.sum[qy, top, :] + g.l1[qy, top, :].astype(F32) + g.lx[1].astype(F32)).astype(BF16)
        c1 = rcopy(g.ty, g.my, ypeer)
        y1.wait_recv()
        g.tx[...] = (b.sum[qx, low, :] + g.l1[qx, low, :].astype(F32) + g.ly[1].astype(F32)).astype(BF16)
        c2 = rcopy(g.tx, g.mx, xpeer)
        return x0, y0, c1, c2

    def reduce_end(cores, cps, out):
        g = sets[3]
        cores[3].wait_recv()
        arrive(cps)
        for rows, near, far_ref in ((top, g.lx, g.my), (low, g.ly, g.mx)):
            out[rows, :] = (
                b.sum[q0, rows, :]
                + g.l1[q0, rows, :].astype(F32)
                + near[0].astype(F32)
                + far_ref[...].astype(F32)
            ).astype(BF16)

    def weight_grad(w, lhs, rhs, gained, first):
        grad = tn(lhs[...].reshape(count, cols), rhs[...].reshape(count, width))
        if gained:
            part = jnp.sum(grad * b.wt[w].reshape(cols, width).astype(F32), axis=0, keepdims=True)
            b.vv[...] = part if first else b.vv[...] + part
            grad = grad * b.gl[...]
        b.gws[w] = grad.astype(BF16).reshape(depth, hl, width)

    def weight_send(w, at):
        return z_scatter(
            lambda q: b.gws.at[w, q, at], lambda k: b.gwl.at[w, k, at], b.gwx.at[w, at]
        )

    def weight_sum(w, st, at):
        gout[w, y, at, :] = z_sum(st, b.gws[w, f, at, :].astype(F32)).astype(BF16)
        return same(gout.at[w, y, at], ypeer)

    every = pl.ds(0, hl)

    weight_grad(2, b.go, b.db, False, False)
    zgo = z_direct(weight_send(2, every))
    weight_grad(1, b.dg, b.nb, True, True)
    zgg = z_direct(weight_send(1, every))
    bone = reduce_begin(lambda pick: nn(pick(b.go), b.wt[2].reshape(cols, width)))

    def backward_pair(j, carry):
        k = SLOT // 2 - 1 - j
        ats = [pl.ds(2 * k + i, 8, stride=SLOT) for i in range(2)]
        size = [[b.dt[e, at, :] for e in range(2)] for at in ats]
        conv = [[b.xc[e, at, :] for e in range(2)] for at in ats]
        dmix = [[b.dm[e, at, :] for e in range(2)] for at in ats]
        push = [jnp.concatenate([size[i][e] * conv[i][e] for i in range(2)], axis=0).astype(BF16) for e in range(2)]
        dlow = [jnp.concatenate([dmix[i][e] for i in range(2)], axis=0).astype(BF16) for e in range(2)]
        rate_sum = [[zero, zero], [zero, zero]]
        weighted = [[zero, zero], [zero, zero]]
        new = []
        for n in range(STATE):
            inm = [b.bc[2 * k + i, n] for i in range(2)]
            outm = [b.bc[2 * k + i, STATE + n] for i in range(2)]
            dins, douts = [], []
            for e in range(2):
                rate = b.rate[n, e]
                here = b.sall[k + 1, n, e]
                before = [b.sall[k, n, e].astype(F32)[8:16], here.astype(F32)[0:8]]
                back = carry[2 * n + e]
                lams = [None, None]
                acc = b.ga[n, e]
                for i in (1, 0):
                    lam = outm[i] * dmix[i][e] + back
                    back = jnp.exp2(size[i][e] * rate) * lam
                    grad = back * before[i]
                    rate_sum[i][e] = rate_sum[i][e] + grad * rate
                    weighted[i][e] = weighted[i][e] + lam * inm[i]
                    acc = acc + grad * size[i][e]
                    lams[i] = lam
                b.ga[n, e] = acc
                new.append(back)
                dins.append(jnp.concatenate(lams, axis=0).astype(BF16) * push[e])
                douts.append(dlow[e] * here)
            b.sall[k + 1, n, 0] = dins[0] + dins[1]
            b.sall[k + 1, n, 1] = douts[0] + douts[1]
        for i in range(2):
            for e in range(2):
                b.ys[e, ats[i], :] = rate_sum[i][e] * LN2 + conv[i][e] * weighted[i][e]
                b.xc[e, ats[i], :] = size[i][e] * weighted[i][e]
        return tuple(new)

    carry = tuple(zero for _ in range(2 * STATE))
    carry = lax.fori_loop(0, SLOT // 8, backward_pair, carry)
    z_absorb(zgo)
    btwo = reduce_second(bone)
    carry = lax.fori_loop(SLOT // 8, 3 * SLOT // 8, backward_pair, carry)
    z_absorb(zgg)
    bthree = reduce_third(btwo)
    carry = lax.fori_loop(3 * SLOT // 8, SLOT // 2, backward_pair, carry)

    parts = [b.sall[1:, n, k].reshape(count, 128) for k in range(2) for n in range(STATE)]
    b.tm[...] = nt(jnp.concatenate(parts, axis=1), b.sel[0:128, :])

    b.t1[...] = nn(b.slow[...], b.wst[...])

    @pl.loop(0, 8)
    def _(j):
        at = slot_rows(j)
        dpre = pair(b.ys, at) * sigmoid(b.t1[at, :] + sbias)
        b.sg[BIAS_ROW : BIAS_ROW + 1, :] += jnp.sum(dpre, axis=0, keepdims=True)
        b.dsl[j] = dpre.astype(BF16)

    b.pp[...] = nt(b.dsl[...].reshape(count, cols), b.wst[...]).reshape(4, 2, SLOT, 128)

    @pl.loop(0, 4)
    def _(q):
        for cc in range(2):
            b.pp[q, cc] += b.tm[pl.ds(2 * q + cc, SLOT, stride=8), :]

    hold = [None, None]

    def pump_second(stage):
        if stage == 0:
            grad = tn(b.slow[...], b.dsl[...].reshape(count, cols))
            b.sg[STEP_ROW:LOG_ROW, :] = grad[:RANK]
        if stage == 1:
            reduce_end(bone, bthree, bsum)
            for n in range(STATE):
                parts = [jnp.sum(b.ga[n, e] * b.rate[n, e], axis=0, keepdims=True) for e in range(2)]
                b.sg[LOG_ROW + n : LOG_ROW + n + 1, :] = jnp.concatenate(parts, axis=1) * LN2
        if stage == 2:
            hold[0] = weight_sum(2, zgo, every)
        if stage == 3:
            hold[1] = weight_sum(1, zgg, every)

    all_reduce(2, pump_second)

    @pl.loop(0, 4)
    def _(q):
        for cc, src in ((c, sets[2].own), (oc, sets[2].oth)):
            b.dpj[slot_rows(2 * q + cc), :] = src[q].astype(BF16)

    b.t1[...] = nn(b.dpj[...], b.wpt[...])

    @pl.loop(0, 4)
    def _(q):
        for cc in range(2):
            j = 2 * q + cc
            at = slot_rows(j)
            dconv = pair(b.xc, at) + pair(b.dm, at) * skip + b.t1[at, :]
            cpre = convolved(j)
            sig = sigmoid(cpre)
            dpre = dconv * (sig * (1.0 + cpre * (1.0 - sig)))
            b.dcp[0:SLOT, :] = dpre
            sums = [jnp.sum(dpre * b.ip[j, 5 + k : 5 + k + SLOT, :], axis=0, keepdims=True) for k in range(CONV)]
            sums.append(jnp.sum(dpre, axis=0, keepdims=True))
            b.sg[TAP_ROW : CONV_ROW + 1, :] += jnp.concatenate(sums, axis=0)
            dinner = taps[CONV - 1] * dpre
            for k in range(CONV - 1):
                dinner = dinner + taps[k] * b.dcp[CONV - 1 - k : CONV - 1 - k + SLOT, :]
            b.di[q, cc] = dinner.astype(BF16)

    weight_grad(0, b.di, b.nb, True, False)
    first, second = pl.ds(0, hl // 2), pl.ds(hl // 2, hl // 2)
    zgi = [weight_send(0, first), weight_send(0, second)]
    for st in zgi:
        z_direct(st)
    for i in range(8):
        b.vs[0, i : i + 1, :] = b.vv[:, i * 128 : i * 128 + 128]
    v1 = rcopy(b.vs.at[0], b.vl.at[0], xpeer)
    settle([*bone, *btwo, *bthree[2:]])
    done = reduce_begin(lambda pick: nn(pick(b.di), b.ws[0]) + nn(pick(b.dg), b.ws[1]))
    v1.wait_recv()
    b.vs[1] = b.vs[0] + b.vl[0]
    v2 = rcopy(b.vs.at[1], b.vl.at[1], ypeer)
    dtwo = reduce_second(done)
    z_absorb(zgi[0])
    z_absorb(zgi[1])
    grad = tn(b.dpj[...], b.cl[...].reshape(count, cols))
    b.sg[0:PROJ, :] = grad[:PROJ]
    for i in range(depth):
        b.sgs[i] = folded(b.sg[:, i * hl : (i + 1) * hl], hl)
    zgs = z_direct(z_scatter(lambda q: b.sgs.at[q], lambda k: b.sgl.at[k], b.sgx))
    v2.wait_recv()
    b.vs[2] = b.vs[1] + b.vl[1]
    v3 = rcopy(b.vs.at[2], b.vl.at[2], core)
    dthree = reduce_third(dtwo)
    v3.wait_recv()
    b.vz[f] = b.vs[2] + b.vl[2]
    v4 = z_gather(lambda q: b.vz.at[q])
    yin = [weight_sum(0, zgi[0], first)]
    z_absorb(zgs)
    yin.append(weight_sum(0, zgi[1], second))
    sout[y] = z_sum(zgs, b.sgs[f].astype(F32)).astype(BF16)
    ysmall = same(sout.at[y], ypeer)
    z_relay(v4)
    reduce_end(done, dthree, dsc)
    z_arrive(v4)
    total = b.vz[0]
    for k in range(1, depth):
        total = total + b.vz[k]
    vout[...] = total
    arrive(hold + yin + [ysmall])
    for cp in started:
        cp.wait_send()


def last_kernel(hl, piece, tok, cot, lens, bsum, dsc, gout, sout, vout, *outs):
    (out, dtok, ggain, ginner, ggate, gconv, gcb, gproj, gstep, gsb, glog, gskip, gwout) = outs
    s = lax.axis_index("shard")
    t32 = tok[...].astype(F32)
    rowid = lax.broadcasted_iota(jnp.int32, (SLOT, 1), 0)
    out[...] = (t32 + jnp.where(rowid < lens[0], bsum[...].astype(F32), 0.0)).astype(BF16)
    inv = lax.rsqrt(jnp.mean(t32 * t32, axis=1, keepdims=True) + EPS)
    ds = dsc[...].astype(F32)
    mean = jnp.mean(ds * t32, axis=1, keepdims=True)
    dtok[...] = cot[...].astype(F32) + inv * ds - t32 * (inv * inv * inv * mean)
    width = tok.shape[1]
    el = 2 * hl
    ginner[...] = gout[0].reshape(el, width).T.astype(F32)
    ggate[...] = gout[1].reshape(el, width).T.astype(F32)
    gwout[...] = gout[2].reshape(el, width).astype(F32)
    small = sout[...].astype(F32)
    halves = [jnp.concatenate([small[k][:, :hl], small[k][:, hl:el]], axis=0) for k in range(2)]
    both = jnp.concatenate(halves, axis=1)
    gproj[...] = both[:PROJ]
    gstep[...] = both[STEP_ROW:LOG_ROW]
    glog[...] = both[LOG_ROW:TAP_ROW]
    gconv[...] = both[TAP_ROW:CONV_ROW]
    gcb[...] = both[CONV_ROW : CONV_ROW + 1].reshape(el)
    gsb[...] = both[BIAS_ROW : BIAS_ROW + 1].reshape(el)
    gskip[...] = both[SKIP_ROW : SKIP_ROW + 1].reshape(el)
    per = 128 // piece
    vec = vout[...]
    rows = lax.broadcasted_iota(jnp.int32, (8, 128), 0)
    row = jnp.sum(jnp.where(rows == s // per, vec, 0.0), axis=0, keepdims=True)
    pick = jnp.zeros((1, piece), F32)
    for i in range(per):
        pick = jnp.where(lax.rem(s, per) == i, row[:, i * piece : (i + 1) * piece], pick)
    ggain[...] = pick.reshape(piece)


def make_local(replicas, shards):
    depth = shards // 4

    def local(
        tokens, norm_gain, w_inner, w_gate, conv_weight, conv_bias, w_proj, w_step, step_bias, a_log, skip_gain,
        w_out, cotangent, lengths,
    ):
        width = tokens.shape[1]
        el = w_inner.shape[1]
        hl = el // 2
        piece = norm_gain.shape[0]
        spec = buffers(depth, hl, width, shards, piece)
        nsem = 96 + 16 * depth
        vm = pl.BlockSpec(memory_space=pltpu.VMEM)
        sm = pl.BlockSpec(memory_space=pltpu.SMEM)
        sds = jax.ShapeDtypeStruct
        mid = pl.pallas_call(
            functools.partial(main_kernel, [tuple(group) for group in spec], depth, hl, piece, nsem),
            out_shape=(
                pltpu.VMEM((SLOT, width), BF16),
                pltpu.VMEM((SLOT, width), BF16),
                pltpu.VMEM((3, 2, hl, width), BF16),
                pltpu.VMEM((2, PACK // 2, 128), BF16),
                pltpu.VMEM((8, 128), F32),
            ),
            in_specs=[vm] * 13 + [sm],
            out_specs=(vm,) * 5,
            scratch_shapes=[pltpu.VMEM(shape, kind) for group in spec for shape, kind in group.values()]
            + [pltpu.SemaphoreType.DMA((nsem,)), pltpu.SemaphoreType.DMA((nsem,))],
            compiler_params=pltpu.CompilerParams(
                collective_id=0, has_side_effects=True, vmem_limit_bytes=61 << 20
            ),
            name="layer",
        )(
            tokens, cotangent, w_inner, w_gate, w_out, w_proj.T, w_step, a_log, conv_weight, conv_bias, step_bias,
            skip_gain, norm_gain, lengths,
        )
        bsum, dsc, gout, sout, vout = mid
        if replicas > 2:
            groups = [[r for r in range(replicas) if r % 2 == k] for k in range(2)]
            gout, sout, vout = (
                lax.psum(v.astype(F32), "replica", axis_index_groups=groups) for v in (gout, sout, vout)
            )
        outs = pl.pallas_call(
            functools.partial(last_kernel, hl, piece),
            out_shape=(
                sds((SLOT, width), BF16),
                sds((SLOT, width), F32),
                sds((piece,), F32),
                sds((width, el), F32),
                sds((width, el), F32),
                sds((CONV, el), F32),
                sds((el,), F32),
                sds((PROJ, el), F32),
                sds((RANK, el), F32),
                sds((el,), F32),
                sds((STATE, el), F32),
                sds((el,), F32),
                sds((el, width), F32),
            ),
            in_specs=[vm, vm, sm] + [vm] * 5,
            out_specs=(vm,) * 13,
            compiler_params=pltpu.CompilerParams(vmem_limit_bytes=16 << 20),
            name="results",
        )(tokens, cotangent, lengths, bsum, dsc, gout, sout, vout)
        return outs[:7] + (outs[7].T,) + outs[8:]

    return local


def solution(mesh):
    return jax.shard_map(
        make_local(mesh.shape["replica"], mesh.shape["shard"]),
        mesh=mesh,
        in_specs=(
            P(("replica", "shard"), None),
            P("shard"),
            P(None, "shard"),
            P(None, "shard"),
            P(None, "shard"),
            P("shard"),
            P("shard", None),
            P(None, "shard"),
            P("shard"),
            P(None, "shard"),
            P("shard"),
            P("shard", None),
            P(("replica", "shard"), None),
            P(("replica", "shard")),
        ),
        out_specs=(
            P(("replica", "shard"), None),
            P(("replica", "shard"), None),
            P("shard"),
            P(None, "shard"),
            P(None, "shard"),
            P(None, "shard"),
            P("shard"),
            P("shard", None),
            P(None, "shard"),
            P("shard"),
            P(None, "shard"),
            P("shard"),
            P("shard", None),
        ),
        check_vma=False,
    )
```

time: 131 us -> 111 us (0.85)
  Pallas kernels: 123 us -> 110 us
  local copies, waits for them, and re-layouts: 6.36 us -> 0.01 us
    pallas_call x1, Pallas kernels: 119 us -> 108 us  [local(): pl.pallas_call(functools.partial(main_kernel, [tuple(group) for group in...]
    unnamed x2 -> x4, local copies, waits for them, and re-layouts: 3 us -> 0.01 us
    concatenate x1 -> x0, local copies, waits for them, and re-layouts: 2.14 us -> none  [local(): jnp.concatenate([w_step, a_log, conv_weight, conv_bias[None], step_bias[N...]
    pallas_call x1, Pallas kernels: 3.72 us -> 1.83 us  [local(): pl.pallas_call(functools.partial(last_kernel, hl, piece), out_shape=(sds(...]
where the time goes in v2:
time: 111 us
  Pallas kernels  110 us (99%)
  between operations  1.34 us (1%)
    pallas_call x1, Pallas kernels, local(): pl.pallas_call(functools.partial(main_kernel, [tuple(group) for group in...  108 us

profile of v2, /device:TPU:0, one launch (start us, length us, event | category | flops | bytes accessed | tf_op | source)
XLA Modules:
  0.0 111.3 jit_solution(13774842503478768261)
XLA Ops:
  1.3 0.0 copy-start
  1.3 0.0 copy-start.1
  1.3 108.1 %layer.1 = (bf16[128,1024]{1,0:T(8,128)(2,1)S(1)}, bf16[128,1024]{1,0:T(8,128)(2,1)S(1)}, bf16[3,2,64,1024]{3,2,1,0:T(8,128)(2,1)S(1)}, bf16[2,96,128]{2,1,0:T(8,128)(2,1)S(1)}, f32[8,128]{1,0:T(8,128)S(1)}) custom-call(bf16[128,1024]{1,0:T(8,128)(2,1)} %tok.1, bf16[128,1024]{1,0:T(8,128)(2,1)} %cot.1, bf16[1024,128]{1,0:T(8,128)(2,1)} %refs_2_.1, ...), custom_call_target="tpu_custom_call" | custom-call | tf_op jit(solution)/shard_map/layer/pallas_call | solution.py:872
  109.4 0.0 copy-done
  109.5 0.0 copy-done.1
  109.5 1.8 %results.1 = (bf16[128,1024]{1,0:T(8,128)(2,1)}, f32[128,1024]{1,0:T(8,128)}, f32[64]{0:T(128)}, f32[1024,128]{1,0:T(8,128)}, f32[1024,128]{1,0:T(8,128)}, /*ind...) custom-call(bf16[128,1024]{1,0:T(8,128)(2,1)S(1)} %copy-done, ...), custom_call_target="tpu_custom_call" | custom-call | tf_op jit(solution)/shard_map/results/pallas_call | solution.py:899
Async XLA Ops:
  1.3 108.2 %copy-start = (bf16[128,1024]{1,0:T(8,128)(2,1)S(1)}, bf16[128,1024]{1,0:T(8,128)(2,1)}, u32[]{:S(2)}) copy-start(bf16[128,1024]{1,0:T(8,128)(2,1)} %tok.1) | copy-start | bytes 786436
  1.3 108.2 %copy-start.1 = (bf16[128,1024]{1,0:T(8,128)(2,1)S(1)}, bf16[128,1024]{1,0:T(8,128)(2,1)}, u32[]{:S(2)}) copy-start(bf16[128,1024]{1,0:T(8,128)(2,1)} %cot.1) | copy-start | bytes 786436

commit v3 on v2

--- a/solution.py
+++ b/solution.py
@@ -99,6 +99,7 @@
         ys=((2, rows, 128), F32),
         dm=((2, rows, 128), F32),
         ga=((STATE, 2, 8, 128), F32),
+        carried=((STATE, 2, 8, 128), F32),
         go=((4, 2, SLOT, cols), BF16),
         dg=((4, 2, SLOT, cols), BF16),
         di=((4, 2, SLOT, cols), BF16),
@@ -383,8 +384,6 @@
     z_relay(zsmall)
     nstate = plane_forward(b.nb, nstate)
     z_relay(zin)
-    zgate = z_gather(lambda q: b.wt.at[1, q])
-    zout = z_gather(lambda q: b.wt.at[2, q])
     z_arrive(zsmall)
     locs = [unfolded(b.pka[i].astype(F32), hl) for i in range(depth)]
     pkl = jnp.concatenate(locs, axis=1)
@@ -420,7 +419,8 @@
     b.gl[...] = jnp.concatenate(pieces, axis=1)
 
     z_arrive(zin)
-    z_relay(zgate)
+    zgate = z_gather(lambda q: b.wt.at[1, q])
+    zout = z_gather(lambda q: b.wt.at[2, q])
 
     def scaled(w):
         full = b.wt[w].reshape(cols, width).astype(F32)
@@ -496,10 +496,9 @@
     dhold = [dstate]
 
     def pump_first(stage):
-        if stage == 1:
-            z_relay(zout)
         if stage == 2:
             dhold[0] = plane_forward(b.db, dhold[0])
+            z_relay(zgate)
         if stage == 3:
             dhold[0] = plane_core(b.db, dhold[0])
 
@@ -528,34 +527,38 @@
     for i in range(2 * STATE):
         b.bc[:, i] = both[:, i * 128 : i * 128 + 128].reshape(SLOT, 8, 128)
 
+    z_relay(zout)
     dstate = plane_last(b.db, dhold[0])
     zero = jnp.zeros((8, 128), F32)
 
-    def forward_pair(k, carry):
-        ats = [pl.ds(2 * k + i, 8, stride=SLOT) for i in range(2)]
+    steps = 4
+
+    def forward_steps(j, carry):
+        base = steps * j
+        ats = [pl.ds(base + i, 8, stride=SLOT) for i in range(steps)]
         size = [[b.dt[e, at, :] for e in range(2)] for at in ats]
-        push = [[size[i][e] * b.xc[e, ats[i], :] for e in range(2)] for i in range(2)]
-        out = [[zero, zero], [zero, zero]]
-        new = []
+        push = [[size[i][e] * b.xc[e, ats[i], :] for e in range(2)] for i in range(steps)]
+        out = [[zero, zero] for _ in range(steps)]
         for n in range(STATE):
-            inm = [b.bc[2 * k + i, n] for i in range(2)]
-            outm = [b.bc[2 * k + i, STATE + n] for i in range(2)]
             for e in range(2):
                 rate = b.rate[n, e]
-                state = carry[2 * n + e]
+                state = b.carried[n, e]
                 kept = []
-                for i in range(2):
-                    state = jnp.exp2(size[i][e] * rate) * state + push[i][e] * inm[i]
-                    out[i][e] = out[i][e] + outm[i] * state
+                for i in range(steps):
+                    state = jnp.exp2(size[i][e] * rate) * state + push[i][e] * b.bc[base + i, n]
+                    out[i][e] = out[i][e] + b.bc[base + i, STATE + n] * state
                     kept.append(state)
-                b.sall[k + 1, n, e] = jnp.concatenate(kept, axis=0).astype(BF16)
-                new.append(state)
-        for i in range(2):
+                b.carried[n, e] = state
+                for p in range(steps // 2):
+                    both_states = jnp.concatenate(kept[2 * p : 2 * p + 2], axis=0)
+                    b.sall[(steps // 2) * j + p + 1, n, e] = both_states.astype(BF16)
+        for i in range(steps):
             for e in range(2):
                 b.ys[e, ats[i], :] = out[i][e]
-        return tuple(new)
-
-    lax.fori_loop(0, SLOT // 2, forward_pair, tuple(zero for _ in range(2 * STATE)))
+        return carry
+
+    b.carried[...] = jnp.zeros((STATE, 2, 8, 128), F32)
+    lax.fori_loop(0, SLOT // steps, forward_steps, 0)
 
     arrive(dstate)
     z_arrive(zgate)
@@ -581,16 +584,21 @@
             b.dg[q, cc] = (dgat * mixed * slope).astype(BF16)
             b.sg[SKIP_ROW : SKIP_ROW + 1, :] += jnp.sum(dmix * conv, axis=0, keepdims=True)
 
-    def reduce_begin(dots):
+    def reduce_begin(dots, more):
         g = sets[3]
-        g.s1[qd] = dots(lambda ref: ref[qd, oc]).astype(BF16)
+
+        def low_of(value, q):
+            return (value + g.s1[q].astype(F32) if more else value).astype(BF16)
+
+        g.s1[qd] = low_of(dots(lambda ref: ref[qd, oc]), qd)
         cores = [rcopy(g.s1.at[qd], g.l1.at[qd], core)]
         others = (qx, qy, q0)
-        rest = dots(lambda ref: jnp.concatenate([ref[q, oc] for q in others], axis=0)).astype(BF16)
+        rest = dots(lambda ref: jnp.concatenate([ref[q, oc] for q in others], axis=0))
         for k, q in enumerate(others):
-            g.s1[q] = rest[k * SLOT : (k + 1) * SLOT]
+            g.s1[q] = low_of(rest[k * SLOT : (k + 1) * SLOT], q)
             cores.append(rcopy(g.s1.at[q], g.l1.at[q], core))
-        b.sum[...] = dots(lambda ref: ref[:, c].reshape(4 * SLOT, cols)).reshape(4, SLOT, width)
+        mine = dots(lambda ref: ref[:, c].reshape(4 * SLOT, cols)).reshape(4, SLOT, width)
+        b.sum[...] = b.sum[...] + mine if more else mine
         return cores
 
     def reduce_second(cores):
@@ -635,13 +643,13 @@
                 + far_ref[...].astype(F32)
             ).astype(BF16)
 
-    def weight_grad(w, lhs, rhs, gained, first):
+    def weight_grad(w, lhs, rhs, gained):
         grad = tn(lhs[...].reshape(count, cols), rhs[...].reshape(count, width))
-        if gained:
-            part = jnp.sum(grad * b.wt[w].reshape(cols, width).astype(F32), axis=0, keepdims=True)
-            b.vv[...] = part if first else b.vv[...] + part
-            grad = grad * b.gl[...]
-        b.gws[w] = grad.astype(BF16).reshape(depth, hl, width)
+        b.gws[w] = (grad * b.gl[...] if gained else grad).astype(BF16).reshape(depth, hl, width)
+        return grad
+
+    def gain_grad(w, grad):
+        return jnp.sum(grad * b.wt[w].reshape(cols, width).astype(F32), axis=0, keepdims=True)
 
     def weight_send(w, at):
         return z_scatter(
@@ -654,11 +662,12 @@
 
     every = pl.ds(0, hl)
 
-    weight_grad(2, b.go, b.db, False, False)
+    weight_grad(2, b.go, b.db, False)
     zgo = z_direct(weight_send(2, every))
-    weight_grad(1, b.dg, b.nb, True, True)
+    grad = weight_grad(1, b.dg, b.nb, True)
     zgg = z_direct(weight_send(1, every))
-    bone = reduce_begin(lambda pick: nn(pick(b.go), b.wt[2].reshape(cols, width)))
+    b.vv[...] = gain_grad(1, grad)
+    bone = reduce_begin(lambda pick: nn(pick(b.go), b.wt[2].reshape(cols, width)), False)
 
     def backward_pair(j, carry):
         k = SLOT // 2 - 1 - j
@@ -731,6 +740,7 @@
             b.pp[q, cc] += b.tm[pl.ds(2 * q + cc, SLOT, stride=8), :]
 
     hold = [None, None]
+    gate_dot = lambda pick: nn(pick(b.dg), b.ws[1])
 
     def pump_second(stage):
         if stage == 0:
@@ -741,8 +751,20 @@
             for n in range(STATE):
                 parts = [jnp.sum(b.ga[n, e] * b.rate[n, e], axis=0, keepdims=True) for e in range(2)]
                 b.sg[LOG_ROW + n : LOG_ROW + n + 1, :] = jnp.concatenate(parts, axis=1) * LN2
+
+            @pl.loop(0, 8)
+            def _(j):
+                at = slot_rows(j)
+                cpre = convolved(j)
+                sig = sigmoid(cpre)
+                b.t2[at, :] = sig * (1.0 + cpre * (1.0 - sig))
+                unpair(b.dm, at, pair(b.xc, at) + pair(b.dm, at) * skip)
+
         if stage == 2:
             hold[0] = weight_sum(2, zgo, every)
+            settle([*bone, *btwo, *bthree[2:]])
+            sets[3].s1[...] = gate_dot(lambda ref: ref[:, oc].reshape(4 * SLOT, cols)).astype(BF16).reshape(4, SLOT, width)
+            b.sum[...] = gate_dot(lambda ref: ref[:, c].reshape(4 * SLOT, cols)).reshape(4, SLOT, width)
         if stage == 3:
             hold[1] = weight_sum(1, zgg, every)
 
@@ -760,10 +782,7 @@
         for cc in range(2):
             j = 2 * q + cc
             at = slot_rows(j)
-            dconv = pair(b.xc, at) + pair(b.dm, at) * skip + b.t1[at, :]
-            cpre = convolved(j)
-            sig = sigmoid(cpre)
-            dpre = dconv * (sig * (1.0 + cpre * (1.0 - sig)))
+            dpre = (pair(b.dm, at) + b.t1[at, :]) * b.t2[at, :]
             b.dcp[0:SLOT, :] = dpre
             sums = [jnp.sum(dpre * b.ip[j, 5 + k : 5 + k + SLOT, :], axis=0, keepdims=True) for k in range(CONV)]
             sums.append(jnp.sum(dpre, axis=0, keepdims=True))
@@ -773,16 +792,16 @@
                 dinner = dinner + taps[k] * b.dcp[CONV - 1 - k : CONV - 1 - k + SLOT, :]
             b.di[q, cc] = dinner.astype(BF16)
 
-    weight_grad(0, b.di, b.nb, True, False)
+    grad = weight_grad(0, b.di, b.nb, True)
     first, second = pl.ds(0, hl // 2), pl.ds(hl // 2, hl // 2)
     zgi = [weight_send(0, first), weight_send(0, second)]
     for st in zgi:
         z_direct(st)
+    total = b.vv[...] + gain_grad(0, grad)
     for i in range(8):
-        b.vs[0, i : i + 1, :] = b.vv[:, i * 128 : i * 128 + 128]
+        b.vs[0, i : i + 1, :] = total[:, i * 128 : i * 128 + 128]
     v1 = rcopy(b.vs.at[0], b.vl.at[0], xpeer)
-    settle([*bone, *btwo, *bthree[2:]])
-    done = reduce_begin(lambda pick: nn(pick(b.di), b.ws[0]) + nn(pick(b.dg), b.ws[1]))
+    done = reduce_begin(lambda pick: nn(pick(b.di), b.ws[0]), True)
     v1.wait_recv()
     b.vs[1] = b.vs[0] + b.vl[0]
     v2 = rcopy(b.vs.at[1], b.vl.at[1], ypeer)

time: 111 us -> 103 us (0.928)
  Pallas kernels: 110 us -> 102 us
    pallas_call x1, Pallas kernels: 108 us -> 100 us  [local(): pl.pallas_call(functools.partial(main_kernel, [tuple(group) for group in...]
where the time goes in v3:
time: 103 us
  Pallas kernels  102 us (99%)
  between operations  1.34 us (1%)
    pallas_call x1, Pallas kernels, local(): pl.pallas_call(functools.partial(main_kernel, [tuple(group) for group in...  100 us

profile of v3, /device:TPU:0, one launch (start us, length us, event | category | flops | bytes accessed | tf_op | source)
XLA Modules:
  0.0 103.3 jit_solution(13596054521312045850)
XLA Ops:
  1.3 0.0 copy-start
  1.3 0.0 copy-start.1
  1.3 100.1 %layer.1 = (bf16[128,1024]{1,0:T(8,128)(2,1)S(1)}, bf16[128,1024]{1,0:T(8,128)(2,1)S(1)}, bf16[3,2,64,1024]{3,2,1,0:T(8,128)(2,1)S(1)}, bf16[2,96,128]{2,1,0:T(8,128)(2,1)S(1)}, f32[8,128]{1,0:T(8,128)S(1)}) custom-call(bf16[128,1024]{1,0:T(8,128)(2,1)} %tok.1, bf16[128,1024]{1,0:T(8,128)(2,1)} %cot.1, bf16[1024,128]{1,0:T(8,128)(2,1)} %refs_2_.1, ...), custom_call_target="tpu_custom_call" | custom-call | tf_op jit(solution)/shard_map/layer/pallas_call | solution.py:891
  101.4 0.0 copy-done
  101.4 0.0 copy-done.1
  101.5 1.8 %results.1 = (bf16[128,1024]{1,0:T(8,128)(2,1)}, f32[128,1024]{1,0:T(8,128)}, f32[64]{0:T(128)}, f32[1024,128]{1,0:T(8,128)}, f32[1024,128]{1,0:T(8,128)}, /*ind...) custom-call(bf16[128,1024]{1,0:T(8,128)(2,1)S(1)} %copy-done, ...), custom_call_target="tpu_custom_call" | custom-call | tf_op jit(solution)/shard_map/results/pallas_call | solution.py:918
Async XLA Ops:
  1.3 100.1 %copy-start = (bf16[128,1024]{1,0:T(8,128)(2,1)S(1)}, bf16[128,1024]{1,0:T(8,128)(2,1)}, u32[]{:S(2)}) copy-start(bf16[128,1024]{1,0:T(8,128)(2,1)} %tok.1) | copy-start | bytes 786436
  1.3 100.1 %copy-start.1 = (bf16[128,1024]{1,0:T(8,128)(2,1)S(1)}, bf16[128,1024]{1,0:T(8,128)(2,1)}, u32[]{:S(2)}) copy-start(bf16[128,1024]{1,0:T(8,128)(2,1)} %cot.1) | copy-start | bytes 786436

commit v4 on v3

--- a/solution.py
+++ b/solution.py
@@ -48,16 +48,10 @@
 def buffers(depth, hl, width, shards, piece):
     cols = depth * hl
     rows = 8 * SLOT
-    reduce_small = dict(
-        s1=((4, SLOT, 128), BF16),
-        l1=((4, SLOT, 128), BF16),
-        s2=((4, SLOT, 128), BF16),
-        l2=((4, SLOT, 128), BF16),
-        s3=((4, SLOT, 128), BF16),
-        l3=((4, SLOT, 128), BF16),
-        own=((4, SLOT, 128), F32),
-        oth=((4, SLOT, 128), F32),
-    )
+    def reduce_small(part):
+        low, full = ((4, part, 128), BF16), ((4, part, 128), F32)
+        return dict(s1=low, l1=low, s2=low, l2=low, s3=low, l3=low, own=full, oth=full)
+
     reduce_large = dict(
         s1=((4, SLOT, width), BF16),
         l1=((4, SLOT, width), BF16),
@@ -85,7 +79,8 @@
         wst=((128, cols), BF16),
         rate=((STATE, 2, 8, 128), F32),
         ip=((8, SLOT + 8, cols), F32),
-        dcp=((SLOT + 8, cols), F32),
+        dcp=((8, SLOT + 8, cols), F32),
+        gacc=((cols, width), F32),
         tm=((rows, 128), F32),
         sel=((256, 2 * STATE * 128), BF16),
         bc=((SLOT, 2 * STATE, 8, 128), F32),
@@ -93,8 +88,8 @@
         cl=((8, SLOT, cols), BF16),
         xc=((2, rows, 128), F32),
         pp=((4, 2, SLOT, 128), F32),
-        slow=((rows, 128), BF16),
-        dpj=((rows, 128), BF16),
+        slow=((8, SLOT, 128), BF16),
+        dpj=((8, SLOT, 128), BF16),
         dt=((2, rows, 128), F32),
         ys=((2, rows, 128), F32),
         dm=((2, rows, 128), F32),
@@ -117,7 +112,7 @@
         vl=((3, 8, 128), F32),
         vz=((depth, 8, 128), F32),
     )
-    return [shapes, reduce_small, reduce_small, reduce_large]
+    return [shapes, reduce_small(SLOT), reduce_small(SLOT // 2), reduce_large, reduce_small(SLOT // 2)]
 
 
 def main_kernel(names, depth, hl, piece, nsem, *refs):
@@ -401,7 +396,7 @@
             b.rate[n, et] = jnp.broadcast_to(row[:, et * 128 : et * 128 + 128], (8, 128))
     nstate = plane_core(b.nb, nstate)
     b.ip[:, 0:8, :] = jnp.zeros((8, 8, cols), F32)
-    b.dcp[SLOT : SLOT + 8, :] = jnp.zeros((8, cols), F32)
+    b.dcp[:, SLOT : SLOT + 8, :] = jnp.zeros((8, 8, cols), F32)
     b.ga[...] = jnp.zeros((STATE, 2, 8, 128), F32)
     b.sall[0] = jnp.zeros((STATE, 2, 16, 128), BF16)
     b.sg[...] = jnp.zeros((PACK, cols), F32)
@@ -447,62 +442,67 @@
         ref[0, at, :] = value[:, :128]
         ref[1, at, :] = value[:, 128:]
 
-    def convolved(j):
-        acc = jnp.broadcast_to(cbias, (SLOT, cols))
+    def convolved(j, begin, size):
+        acc = jnp.broadcast_to(cbias, (size, cols))
         for k in range(CONV):
-            acc = acc + taps[k] * b.ip[j, 5 + k : 5 + k + SLOT, :]
+            acc = acc + taps[k] * b.ip[j, 5 + k + begin : 5 + k + begin + size, :]
         return acc
 
     b.ip[:, 8 : 8 + SLOT, :] = nt(b.nb[...].reshape(count, width), b.ws[0]).reshape(8, SLOT, cols)
 
     @pl.loop(0, 8)
     def _(j):
-        acc = convolved(j)
+        acc = convolved(j, 0, SLOT)
         out = acc * sigmoid(acc)
         unpair(b.xc, slot_rows(j), out)
         b.cl[j] = out.astype(BF16)
 
     b.pp[...] = nt(b.cl[...].reshape(count, cols), b.wpt[...]).reshape(4, 2, SLOT, 128)
 
-    def all_reduce(which, between):
+    def all_reduce(which, rows):
         g = sets[which]
-        g.s1[...] = b.pp[:, oc].astype(BF16)
-        one = rcopy(g.s1, g.l1, core)
-        between(0)
-        one.wait_recv()
-        total = b.pp[:, c] + g.l1[...].astype(F32)
-        g.s2[...] = total.astype(BF16)
-        two = [
-            rcopy(g.s2.at[pl.ds(0, 2)], g.l2.at[pl.ds(0, 2)], xpeer),
-            rcopy(g.s2.at[pl.ds(2, 2)], g.l2.at[pl.ds(2, 2)], ypeer),
-        ]
-        g.own[...] = total
-        between(1)
-        arrive(two)
-        total = g.own[...] + g.l2[...].astype(F32)
-        g.s3[...] = total.astype(BF16)
-        three = [
-            rcopy(g.s3.at[pl.ds(0, 2)], g.l3.at[pl.ds(0, 2)], ypeer),
-            rcopy(g.s3.at[pl.ds(2, 2)], g.l3.at[pl.ds(2, 2)], xpeer),
-        ]
-        g.own[...] = total
-        between(2)
-        arrive(three)
-        g.own[...] = g.own[...] + g.l3[...].astype(F32)
-        four = rcopy(g.own, g.oth, core)
-        between(3)
-        four.wait_recv()
-
-    dhold = [dstate]
-
-    def pump_first(stage):
-        if stage == 2:
-            dhold[0] = plane_forward(b.db, dhold[0])
-            z_relay(zgate)
-        if stage == 3:
-            dhold[0] = plane_core(b.db, dhold[0])
-
-    all_reduce(1, pump_first)
+        flight = []
+
+        def first():
+            g.s1[...] = b.pp[:, oc, rows, :].astype(BF16)
+            flight[:] = [rcopy(g.s1, g.l1, core)]
+
+        def second():
+            arrive(flight)
+            total = b.pp[:, c, rows, :] + g.l1[...].astype(F32)
+            g.s2[...] = total.astype(BF16)
+            flight[:] = [
+                rcopy(g.s2.at[pl.ds(0, 2)], g.l2.at[pl.ds(0, 2)], xpeer),
+                rcopy(g.s2.at[pl.ds(2, 2)], g.l2.at[pl.ds(2, 2)], ypeer),
+            ]
+            g.own[...] = total
+
+        def third():
+            arrive(flight)
+            total = g.own[...] + g.l2[...].astype(F32)
+            g.s3[...] = total.astype(BF16)
+            flight[:] = [
+                rcopy(g.s3.at[pl.ds(0, 2)], g.l3.at[pl.ds(0, 2)], ypeer),
+                rcopy(g.s3.at[pl.ds(2, 2)], g.l3.at[pl.ds(2, 2)], xpeer),
+            ]
+            g.own[...] = total
+
+        def fourth():
+            arrive(flight)
+            g.own[...] = g.own[...] + g.l3[...].astype(F32)
+            flight[:] = [rcopy(g.own, g.oth, core)]
+
+        return [first, second, third, fourth, lambda: arrive(flight)]
+
+    summed = all_reduce(1, slice(0, SLOT))
+    summed[0]()
+    summed[1]()
+    summed[2]()
+    dstate = plane_forward(b.db, dstate)
+    z_relay(zgate)
+    summed[3]()
+    dstate = plane_core(b.db, dstate)
+    summed[4]()
 
     @pl.loop(0, 4)
     def _(q):
@@ -510,9 +510,9 @@
             j = 2 * q + cc
             proj = src[q]
             b.tm[pl.ds(j, SLOT, stride=8), :] = proj
-            b.slow[slot_rows(j), :] = proj.astype(BF16)
-
-    b.t1[...] = nn(b.slow[...], b.wst[...])
+            b.slow[j] = proj.astype(BF16)
+
+    b.t1[...] = nn(b.slow[...].reshape(count, 128), b.wst[...])
 
     @pl.loop(0, 8)
     def _(j):
@@ -528,7 +528,7 @@
         b.bc[:, i] = both[:, i * 128 : i * 128 + 128].reshape(SLOT, 8, 128)
 
     z_relay(zout)
-    dstate = plane_last(b.db, dhold[0])
+    dstate = plane_last(b.db, dstate)
     zero = jnp.zeros((8, 128), F32)
 
     steps = 4
@@ -643,10 +643,12 @@
                 + far_ref[...].astype(F32)
             ).astype(BF16)
 
-    def weight_grad(w, lhs, rhs, gained):
-        grad = tn(lhs[...].reshape(count, cols), rhs[...].reshape(count, width))
+    def weight_grad(w, grad, gained):
         b.gws[w] = (grad * b.gl[...] if gained else grad).astype(BF16).reshape(depth, hl, width)
         return grad
+
+    def rows_grad(lhs, rhs):
+        return tn(lhs[...].reshape(count, cols), rhs[...].reshape(count, width))
 
     def gain_grad(w, grad):
         return jnp.sum(grad * b.wt[w].reshape(cols, width).astype(F32), axis=0, keepdims=True)
@@ -662,9 +664,9 @@
 
     every = pl.ds(0, hl)
 
-    weight_grad(2, b.go, b.db, False)
+    weight_grad(2, rows_grad(b.go, b.db), False)
     zgo = z_direct(weight_send(2, every))
-    grad = weight_grad(1, b.dg, b.nb, True)
+    grad = weight_grad(1, rows_grad(b.dg, b.nb), True)
     zgg = z_direct(weight_send(1, every))
     b.vv[...] = gain_grad(1, grad)
     bone = reduce_begin(lambda pick: nn(pick(b.go), b.wt[2].reshape(cols, width)), False)
@@ -712,87 +714,123 @@
         return tuple(new)
 
     carry = tuple(zero for _ in range(2 * STATE))
-    carry = lax.fori_loop(0, SLOT // 8, backward_pair, carry)
+    carry = lax.fori_loop(0, SLOT // 16, backward_pair, carry)
+    btwo = reduce_second(bone)
+    carry = lax.fori_loop(SLOT // 16, 3 * SLOT // 16, backward_pair, carry)
     z_absorb(zgo)
-    btwo = reduce_second(bone)
-    carry = lax.fori_loop(SLOT // 8, 3 * SLOT // 8, backward_pair, carry)
+    bthree = reduce_third(btwo)
+    carry = lax.fori_loop(3 * SLOT // 16, SLOT // 4, backward_pair, carry)
+
+    def cut_of(h):
+        return slice(h * half, h * half + half)
+
+    def half_rows(j, h):
+        return pl.ds(pl.multiple_of(j * SLOT + h * half, half), half)
+
+    def packed_rows(j, h):
+        return pl.ds(pl.multiple_of(h * 8 * half + j * half, half), half)
+
+    def map_sums(h):
+        begin = 1 + h * half // 2
+        parts = [
+            b.sall[begin : begin + half // 2, n, k].reshape(8 * half, 128) for k in range(2) for n in range(STATE)
+        ]
+        b.tm[h * 8 * half : (h + 1) * 8 * half, :] = nt(jnp.concatenate(parts, axis=1), b.sel[0:128, :])
+
+    def rank_part(h):
+        span = slice(h * 8 * half, (h + 1) * 8 * half)
+        b.t1[span, :] = nn(b.slow[:, cut_of(h), :].reshape(8 * half, 128), b.wst[...])
+
+        @pl.loop(0, 8)
+        def _(j):
+            dpre = pair(b.ys, half_rows(j, h)) * sigmoid(b.t1[packed_rows(j, h), :] + sbias)
+            b.sg[BIAS_ROW : BIAS_ROW + 1, :] += jnp.sum(dpre, axis=0, keepdims=True)
+            b.dsl[j, cut_of(h), :] = dpre.astype(BF16)
+
+        rank = nt(b.dsl[:, cut_of(h), :].reshape(8 * half, cols), b.wst[...])
+        for j in range(8):
+            maps = b.tm[pl.ds(h * 8 * half + j, half, stride=8), :]
+            b.pp[j // 2, j % 2, cut_of(h), :] = rank[j * half : (j + 1) * half] + maps
+
+    def slopes(h):
+        @pl.loop(0, 8)
+        def _(j):
+            at = half_rows(j, h)
+            cpre = convolved(j, h * half, half)
+            sig = sigmoid(cpre)
+            b.t2[at, :] = sig * (1.0 + cpre * (1.0 - sig))
+            unpair(b.dm, at, pair(b.xc, at) + pair(b.dm, at) * skip)
+
+    def inner_part(which, h):
+        @pl.loop(0, 4)
+        def _(q):
+            for cc, src in ((c, sets[which].own), (oc, sets[which].oth)):
+                b.dpj[2 * q + cc, cut_of(h), :] = src[q].astype(BF16)
+
+        span = slice(h * 8 * half, (h + 1) * 8 * half)
+        b.t1[span, :] = nn(b.dpj[:, cut_of(h), :].reshape(8 * half, 128), b.wpt[...])
+
+        @pl.loop(0, 4)
+        def _(q):
+            for cc in range(2):
+                j = 2 * q + cc
+                at = half_rows(j, h)
+                dpre = (pair(b.dm, at) + b.t1[packed_rows(j, h), :]) * b.t2[at, :]
+                b.dcp[j, cut_of(h), :] = dpre
+                sums = []
+                for k in range(CONV):
+                    begin = 5 + k + h * half
+                    sums.append(jnp.sum(dpre * b.ip[j, begin : begin + half, :], axis=0, keepdims=True))
+                sums.append(jnp.sum(dpre, axis=0, keepdims=True))
+                b.sg[TAP_ROW : CONV_ROW + 1, :] += jnp.concatenate(sums, axis=0)
+                dinner = taps[CONV - 1] * dpre
+                for k in range(CONV - 1):
+                    begin = CONV - 1 - k + h * half
+                    dinner = dinner + taps[k] * b.dcp[j, begin : begin + half, :]
+                b.di[q, cc, cut_of(h), :] = dinner.astype(BF16)
+
+    def inner_grad(h):
+        return tn(
+            b.di[:, :, cut_of(h), :].reshape(8 * half, cols), b.nb[:, :, cut_of(h), :].reshape(8 * half, width)
+        )
+
+    map_sums(1)
+    rank_part(1)
+    later = all_reduce(2, cut_of(1))
+    later[0]()
+    marks = [SLOT // 4 + v for v in (0, 8, 24, SLOT // 4)]
+    for k in range(3):
+        carry = lax.fori_loop(marks[k], marks[k + 1], backward_pair, carry)
+        if k < 2:
+            later[k + 1]()
     z_absorb(zgg)
-    bthree = reduce_third(btwo)
-    carry = lax.fori_loop(3 * SLOT // 8, SLOT // 2, backward_pair, carry)
-
-    parts = [b.sall[1:, n, k].reshape(count, 128) for k in range(2) for n in range(STATE)]
-    b.tm[...] = nt(jnp.concatenate(parts, axis=1), b.sel[0:128, :])
-
-    b.t1[...] = nn(b.slow[...], b.wst[...])
-
-    @pl.loop(0, 8)
-    def _(j):
-        at = slot_rows(j)
-        dpre = pair(b.ys, at) * sigmoid(b.t1[at, :] + sbias)
-        b.sg[BIAS_ROW : BIAS_ROW + 1, :] += jnp.sum(dpre, axis=0, keepdims=True)
-        b.dsl[j] = dpre.astype(BF16)
-
-    b.pp[...] = nt(b.dsl[...].reshape(count, cols), b.wst[...]).reshape(4, 2, SLOT, 128)
-
-    @pl.loop(0, 4)
-    def _(q):
-        for cc in range(2):
-            b.pp[q, cc] += b.tm[pl.ds(2 * q + cc, SLOT, stride=8), :]
-
-    hold = [None, None]
-    gate_dot = lambda pick: nn(pick(b.dg), b.ws[1])
-
-    def pump_second(stage):
-        if stage == 0:
-            grad = tn(b.slow[...], b.dsl[...].reshape(count, cols))
-            b.sg[STEP_ROW:LOG_ROW, :] = grad[:RANK]
-        if stage == 1:
-            reduce_end(bone, bthree, bsum)
-            for n in range(STATE):
-                parts = [jnp.sum(b.ga[n, e] * b.rate[n, e], axis=0, keepdims=True) for e in range(2)]
-                b.sg[LOG_ROW + n : LOG_ROW + n + 1, :] = jnp.concatenate(parts, axis=1) * LN2
-
-            @pl.loop(0, 8)
-            def _(j):
-                at = slot_rows(j)
-                cpre = convolved(j)
-                sig = sigmoid(cpre)
-                b.t2[at, :] = sig * (1.0 + cpre * (1.0 - sig))
-                unpair(b.dm, at, pair(b.xc, at) + pair(b.dm, at) * skip)
-
-        if stage == 2:
-            hold[0] = weight_sum(2, zgo, every)
-            settle([*bone, *btwo, *bthree[2:]])
-            sets[3].s1[...] = gate_dot(lambda ref: ref[:, oc].reshape(4 * SLOT, cols)).astype(BF16).reshape(4, SLOT, width)
-            b.sum[...] = gate_dot(lambda ref: ref[:, c].reshape(4 * SLOT, cols)).reshape(4, SLOT, width)
-        if stage == 3:
-            hold[1] = weight_sum(1, zgg, every)
-
-    all_reduce(2, pump_second)
-
-    @pl.loop(0, 4)
-    def _(q):
-        for cc, src in ((c, sets[2].own), (oc, sets[2].oth)):
-            b.dpj[slot_rows(2 * q + cc), :] = src[q].astype(BF16)
-
-    b.t1[...] = nn(b.dpj[...], b.wpt[...])
-
-    @pl.loop(0, 4)
-    def _(q):
-        for cc in range(2):
-            j = 2 * q + cc
-            at = slot_rows(j)
-            dpre = (pair(b.dm, at) + b.t1[at, :]) * b.t2[at, :]
-            b.dcp[0:SLOT, :] = dpre
-            sums = [jnp.sum(dpre * b.ip[j, 5 + k : 5 + k + SLOT, :], axis=0, keepdims=True) for k in range(CONV)]
-            sums.append(jnp.sum(dpre, axis=0, keepdims=True))
-            b.sg[TAP_ROW : CONV_ROW + 1, :] += jnp.concatenate(sums, axis=0)
-            dinner = taps[CONV - 1] * dpre
-            for k in range(CONV - 1):
-                dinner = dinner + taps[k] * b.dcp[CONV - 1 - k : CONV - 1 - k + SLOT, :]
-            b.di[q, cc] = dinner.astype(BF16)
-
-    grad = weight_grad(0, b.di, b.nb, True)
+    map_sums(0)
+    later[3]()
+    rank_part(0)
+    sooner = all_reduce(4, cut_of(0))
+    sooner[0]()
+    later[4]()
+    slopes(1)
+    sooner[1]()
+    inner_part(2, 1)
+    reduce_end(bone, bthree, bsum)
+    for n in range(STATE):
+        parts = [jnp.sum(b.ga[n, e] * b.rate[n, e], axis=0, keepdims=True) for e in range(2)]
+        b.sg[LOG_ROW + n : LOG_ROW + n + 1, :] = jnp.concatenate(parts, axis=1) * LN2
+    slopes(0)
+    sooner[2]()
+    hold = [weight_sum(2, zgo, every)]
+    b.gacc[...] = inner_grad(1)
+    settle([*bone, *btwo, *bthree[2:]])
+    gate_dot = lambda ref: nn(ref.reshape(4 * SLOT, cols), b.ws[1]).reshape(4, SLOT, width)
+    sets[3].s1[...] = gate_dot(b.dg[:, oc]).astype(BF16)
+    b.sum[...] = gate_dot(b.dg[:, c])
+    sooner[3]()
+    hold.append(weight_sum(1, zgg, every))
+    sooner[4]()
+    inner_part(4, 0)
+
+    grad = weight_grad(0, b.gacc[...] + inner_grad(0), True)
     first, second = pl.ds(0, hl // 2), pl.ds(hl // 2, hl // 2)
     zgi = [weight_send(0, first), weight_send(0, second)]
     for st in zgi:
@@ -808,8 +846,10 @@
     dtwo = reduce_second(done)
     z_absorb(zgi[0])
     z_absorb(zgi[1])
-    grad = tn(b.dpj[...], b.cl[...].reshape(count, cols))
+    grad = tn(b.dpj[...].reshape(count, 128), b.cl[...].reshape(count, cols))
     b.sg[0:PROJ, :] = grad[:PROJ]
+    grad = tn(b.slow[...].reshape(count, 128), b.dsl[...].reshape(count, cols))
+    b.sg[STEP_ROW:LOG_ROW, :] = grad[:RANK]
     for i in range(depth):
         b.sgs[i] = folded(b.sg[:, i * hl : (i + 1) * hl], hl)
     zgs = z_direct(z_scatter(lambda q: b.sgs.at[q], lambda k: b.sgl.at[k], b.sgx))

time: 103 us -> 102 us (level)
    pallas_call x1, Pallas kernels: 100 us -> 99 us  [local(): pl.pallas_call(functools.partial(main_kernel, [tuple(group) for group in...]
where the time goes in v4:
time: 102 us
  Pallas kernels  101 us (99%)
  between operations  1.34 us (1%)
    pallas_call x1, Pallas kernels, local(): pl.pallas_call(functools.partial(main_kernel, [tuple(group) for group in...  99 us

profile of v4, /device:TPU:0, one launch (start us, length us, event | category | flops | bytes accessed | tf_op | source)
XLA Modules:
  0.0 102.2 jit_solution(11342414477885841613)
XLA Ops:
  1.3 0.0 copy-start
  1.3 0.0 copy-start.1
  1.3 99.0 %layer.1 = (bf16[128,1024]{1,0:T(8,128)(2,1)S(1)}, bf16[128,1024]{1,0:T(8,128)(2,1)S(1)}, bf16[3,2,64,1024]{3,2,1,0:T(8,128)(2,1)S(1)}, bf16[2,96,128]{2,1,0:T(8,128)(2,1)S(1)}, f32[8,128]{1,0:T(8,128)S(1)}) custom-call(bf16[128,1024]{1,0:T(8,128)(2,1)} %tok.1, bf16[128,1024]{1,0:T(8,128)(2,1)} %cot.1, bf16[1024,128]{1,0:T(8,128)(2,1)} %refs_2_.1, ...), custom_call_target="tpu_custom_call" | custom-call | tf_op jit(solution)/shard_map/layer/pallas_call | solution.py:931
  100.3 0.0 copy-done
  100.3 0.0 copy-done.1
  100.3 1.8 %results.1 = (bf16[128,1024]{1,0:T(8,128)(2,1)}, f32[128,1024]{1,0:T(8,128)}, f32[64]{0:T(128)}, f32[1024,128]{1,0:T(8,128)}, f32[1024,128]{1,0:T(8,128)}, /*ind...) custom-call(bf16[128,1024]{1,0:T(8,128)(2,1)S(1)} %copy-done, ...), custom_call_target="tpu_custom_call" | custom-call | tf_op jit(solution)/shard_map/results/pallas_call | solution.py:958
Async XLA Ops:
  1.3 99.0 %copy-start = (bf16[128,1024]{1,0:T(8,128)(2,1)S(1)}, bf16[128,1024]{1,0:T(8,128)(2,1)}, u32[]{:S(2)}) copy-start(bf16[128,1024]{1,0:T(8,128)(2,1)} %tok.1) | copy-start | bytes 786436
  1.3 99.0 %copy-start.1 = (bf16[128,1024]{1,0:T(8,128)(2,1)S(1)}, bf16[128,1024]{1,0:T(8,128)(2,1)}, u32[]{:S(2)}) copy-start(bf16[128,1024]{1,0:T(8,128)(2,1)} %cot.1) | copy-start | bytes 786436

commit v5 on v4

--- a/solution.py
+++ b/solution.py
@@ -112,7 +112,8 @@
         vl=((3, 8, 128), F32),
         vz=((depth, 8, 128), F32),
     )
-    return [shapes, reduce_small(SLOT), reduce_small(SLOT // 2), reduce_large, reduce_small(SLOT // 2)]
+    part = reduce_small(SLOT // 2)
+    return [shapes, part, part, reduce_large, part, part]
 
 
 def main_kernel(names, depth, hl, piece, nsem, *refs):
@@ -494,41 +495,51 @@
 
         return [first, second, third, fourth, lambda: arrive(flight)]
 
-    summed = all_reduce(1, slice(0, SLOT))
-    summed[0]()
-    summed[1]()
-    summed[2]()
+    def cut_of(h):
+        return slice(h * half, h * half + half)
+
+    def half_rows(j, h):
+        return pl.ds(pl.multiple_of(j * SLOT + h * half, half), half)
+
+    def packed_rows(j, h):
+        return pl.ds(pl.multiple_of(h * 8 * half + j * half, half), half)
+
+    front = all_reduce(1, cut_of(0))
+    back = all_reduce(5, cut_of(1))
+    for k in range(3):
+        front[k]()
+        back[k]()
     dstate = plane_forward(b.db, dstate)
     z_relay(zgate)
-    summed[3]()
+    front[3]()
+    back[3]()
     dstate = plane_core(b.db, dstate)
-    summed[4]()
-
-    @pl.loop(0, 4)
-    def _(q):
-        for cc, src in ((c, sets[1].own), (oc, sets[1].oth)):
-            j = 2 * q + cc
-            proj = src[q]
-            b.tm[pl.ds(j, SLOT, stride=8), :] = proj
-            b.slow[j] = proj.astype(BF16)
-
-    b.t1[...] = nn(b.slow[...].reshape(count, 128), b.wst[...])
-
-    @pl.loop(0, 8)
-    def _(j):
-        at = slot_rows(j)
-        pre = b.t1[at, :] + sbias
-        unpair(b.dt, at, jnp.maximum(pre, 0.0) + jnp.log1p(jnp.exp(-jnp.abs(pre))))
-
-    tm = b.tm[...]
-    high = tm.astype(BF16)
-    spread = jnp.concatenate([high, (tm - high.astype(F32)).astype(BF16)], axis=1)
-    both = nn(spread, b.sel[...])
-    for i in range(2 * STATE):
-        b.bc[:, i] = both[:, i * 128 : i * 128 + 128].reshape(SLOT, 8, 128)
-
-    z_relay(zout)
-    dstate = plane_last(b.db, dstate)
+    front[4]()
+
+    def scan_inputs(which, h):
+        @pl.loop(0, 4)
+        def _(q):
+            for cc, src in ((c, sets[which].own), (oc, sets[which].oth)):
+                j = 2 * q + cc
+                proj = src[q]
+                b.tm[pl.ds(h * 8 * half + j, half, stride=8), :] = proj
+                b.slow[j, cut_of(h), :] = proj.astype(BF16)
+
+        span = slice(h * 8 * half, (h + 1) * 8 * half)
+        b.t1[span, :] = nn(b.slow[:, cut_of(h), :].reshape(8 * half, 128), b.wst[...])
+
+        @pl.loop(0, 8)
+        def _(j):
+            pre = b.t1[packed_rows(j, h), :] + sbias
+            unpair(b.dt, half_rows(j, h), jnp.maximum(pre, 0.0) + jnp.log1p(jnp.exp(-jnp.abs(pre))))
+
+        tm = b.tm[span, :]
+        high = tm.astype(BF16)
+        spread = jnp.concatenate([high, (tm - high.astype(F32)).astype(BF16)], axis=1)
+        both = nn(spread, b.sel[...])
+        for i in range(2 * STATE):
+            b.bc[cut_of(h), i] = both[:, i * 128 : i * 128 + 128].reshape(half, 8, 128)
+
     zero = jnp.zeros((8, 128), F32)
 
     steps = 4
@@ -558,7 +569,13 @@
         return carry
 
     b.carried[...] = jnp.zeros((STATE, 2, 8, 128), F32)
-    lax.fori_loop(0, SLOT // steps, forward_steps, 0)
+    scan_inputs(1, 0)
+    lax.fori_loop(0, half // steps, forward_steps, 0)
+    z_relay(zout)
+    back[4]()
+    scan_inputs(5, 1)
+    dstate = plane_last(b.db, dstate)
+    lax.fori_loop(half // steps, SLOT // steps, forward_steps, 0)
 
     arrive(dstate)
     z_arrive(zgate)
@@ -714,21 +731,12 @@
         return tuple(new)
 
     carry = tuple(zero for _ in range(2 * STATE))
-    carry = lax.fori_loop(0, SLOT // 16, backward_pair, carry)
+    carry = lax.fori_loop(0, SLOT // 16, backward_pair, carry, unroll=2)
     btwo = reduce_second(bone)
-    carry = lax.fori_loop(SLOT // 16, 3 * SLOT // 16, backward_pair, carry)
+    carry = lax.fori_loop(SLOT // 16, 3 * SLOT // 16, backward_pair, carry, unroll=2)
     z_absorb(zgo)
     bthree = reduce_third(btwo)
-    carry = lax.fori_loop(3 * SLOT // 16, SLOT // 4, backward_pair, carry)
-
-    def cut_of(h):
-        return slice(h * half, h * half + half)
-
-    def half_rows(j, h):
-        return pl.ds(pl.multiple_of(j * SLOT + h * half, half), half)
-
-    def packed_rows(j, h):
-        return pl.ds(pl.multiple_of(h * 8 * half + j * half, half), half)
+    carry = lax.fori_loop(3 * SLOT // 16, SLOT // 4, backward_pair, carry, unroll=2)
 
     def map_sums(h):
         begin = 1 + h * half // 2
@@ -798,15 +806,15 @@
     rank_part(1)
     later = all_reduce(2, cut_of(1))
     later[0]()
-    marks = [SLOT // 4 + v for v in (0, 8, 24, SLOT // 4)]
+    marks = [SLOT // 4 + v for v in (0, 8, 26, SLOT // 4)]
     for k in range(3):
-        carry = lax.fori_loop(marks[k], marks[k + 1], backward_pair, carry)
+        carry = lax.fori_loop(marks[k], marks[k + 1], backward_pair, carry, unroll=2)
         if k < 2:
             later[k + 1]()
     z_absorb(zgg)
     map_sums(0)
+    rank_part(0)
     later[3]()
-    rank_part(0)
     sooner = all_reduce(4, cut_of(0))
     sooner[0]()
     later[4]()

time: 102 us -> 101 us (level)
  Pallas kernels: 101 us -> 99.6 us
    pallas_call x1, Pallas kernels: 99 us -> 97.8 us  [local(): pl.pallas_call(functools.partial(main_kernel, [tuple(group) for group in...]
where the time goes in v5:
time: 101 us
  Pallas kernels  99.6 us (99%)
  between operations  1.34 us (1%)
    pallas_call x1, Pallas kernels, local(): pl.pallas_call(functools.partial(main_kernel, [tuple(group) for group in...  97.8 us

profile of v5, /device:TPU:0, one launch (start us, length us, event | category | flops | bytes accessed | tf_op | source)
XLA Modules:
  0.0 101.0 jit_solution(18408842110648062469)
XLA Ops:
  1.3 0.0 copy-start
  1.3 0.0 copy-start.1
  1.3 97.8 %layer.1 = (bf16[128,1024]{1,0:T(8,128)(2,1)S(1)}, bf16[128,1024]{1,0:T(8,128)(2,1)S(1)}, bf16[3,2,64,1024]{3,2,1,0:T(8,128)(2,1)S(1)}, bf16[2,96,128]{2,1,0:T(8,128)(2,1)S(1)}, f32[8,128]{1,0:T(8,128)S(1)}) custom-call(bf16[128,1024]{1,0:T(8,128)(2,1)} %tok.1, bf16[128,1024]{1,0:T(8,128)(2,1)} %cot.1, bf16[1024,128]{1,0:T(8,128)(2,1)} %refs_2_.1, ...), custom_call_target="tpu_custom_call" | custom-call | tf_op jit(solution)/shard_map/layer/pallas_call | solution.py:939
  99.1 0.0 copy-done
  99.1 0.0 copy-done.1
  99.2 1.8 %results.1 = (bf16[128,1024]{1,0:T(8,128)(2,1)}, f32[128,1024]{1,0:T(8,128)}, f32[64]{0:T(128)}, f32[1024,128]{1,0:T(8,128)}, f32[1024,128]{1,0:T(8,128)}, /*ind...) custom-call(bf16[128,1024]{1,0:T(8,128)(2,1)S(1)} %copy-done, ...), custom_call_target="tpu_custom_call" | custom-call | tf_op jit(solution)/shard_map/results/pallas_call | solution.py:966
Async XLA Ops:
  1.3 97.8 %copy-start = (bf16[128,1024]{1,0:T(8,128)(2,1)S(1)}, bf16[128,1024]{1,0:T(8,128)(2,1)}, u32[]{:S(2)}) copy-start(bf16[128,1024]{1,0:T(8,128)(2,1)} %tok.1) | copy-start | bytes 786436
  1.3 97.8 %copy-start.1 = (bf16[128,1024]{1,0:T(8,128)(2,1)S(1)}, bf16[128,1024]{1,0:T(8,128)(2,1)}, u32[]{:S(2)}) copy-start(bf16[128,1024]{1,0:T(8,128)(2,1)} %cot.1) | copy-start | bytes 786436

commit v6 on v5

--- a/solution.py
+++ b/solution.py
@@ -822,12 +822,9 @@
     sooner[1]()
     inner_part(2, 1)
     reduce_end(bone, bthree, bsum)
-    for n in range(STATE):
-        parts = [jnp.sum(b.ga[n, e] * b.rate[n, e], axis=0, keepdims=True) for e in range(2)]
-        b.sg[LOG_ROW + n : LOG_ROW + n + 1, :] = jnp.concatenate(parts, axis=1) * LN2
-    slopes(0)
     sooner[2]()
     hold = [weight_sum(2, zgo, every)]
+    slopes(0)
     b.gacc[...] = inner_grad(1)
     settle([*bone, *btwo, *bthree[2:]])
     gate_dot = lambda ref: nn(ref.reshape(4 * SLOT, cols), b.ws[1]).reshape(4, SLOT, width)
@@ -854,6 +851,9 @@
     dtwo = reduce_second(done)
     z_absorb(zgi[0])
     z_absorb(zgi[1])
+    for n in range(STATE):
+        parts = [jnp.sum(b.ga[n, e] * b.rate[n, e], axis=0, keepdims=True) for e in range(2)]
+        b.sg[LOG_ROW + n : LOG_ROW + n + 1, :] = jnp.concatenate(parts, axis=1) * LN2
     grad = tn(b.dpj[...].reshape(count, 128), b.cl[...].reshape(count, cols))
     b.sg[0:PROJ, :] = grad[:PROJ]
     grad = tn(b.slow[...].reshape(count, 128), b.dsl[...].reshape(count, cols))

time: 101 us -> 101 us (level)
  no operation moved by 1% of the time
where the time goes in v6:
time: 101 us
  Pallas kernels  99.6 us (99%)
  between operations  1.34 us (1%)
    pallas_call x1, Pallas kernels, local(): pl.pallas_call(functools.partial(main_kernel, [tuple(group) for group in...  97.8 us

profile of v6, /device:TPU:0, one launch (start us, length us, event | category | flops | bytes accessed | tf_op | source)
XLA Modules:
  0.0 101.0 jit_solution(6953841544748485617)
XLA Ops:
  1.3 0.0 copy-start
  1.3 0.0 copy-start.1
  1.3 97.8 %layer.1 = (bf16[128,1024]{1,0:T(8,128)(2,1)S(1)}, bf16[128,1024]{1,0:T(8,128)(2,1)S(1)}, bf16[3,2,64,1024]{3,2,1,0:T(8,128)(2,1)S(1)}, bf16[2,96,128]{2,1,0:T(8,128)(2,1)S(1)}, f32[8,128]{1,0:T(8,128)S(1)}) custom-call(bf16[128,1024]{1,0:T(8,128)(2,1)} %tok.1, bf16[128,1024]{1,0:T(8,128)(2,1)} %cot.1, bf16[1024,128]{1,0:T(8,128)(2,1)} %refs_2_.1, ...), custom_call_target="tpu_custom_call" | custom-call | tf_op jit(solution)/shard_map/layer/pallas_call | solution.py:939
  99.1 0.0 copy-done
  99.1 0.0 copy-done.1
  99.2 1.8 %results.1 = (bf16[128,1024]{1,0:T(8,128)(2,1)}, f32[128,1024]{1,0:T(8,128)}, f32[64]{0:T(128)}, f32[1024,128]{1,0:T(8,128)}, f32[1024,128]{1,0:T(8,128)}, /*ind...) custom-call(bf16[128,1024]{1,0:T(8,128)(2,1)S(1)} %copy-done, ...), custom_call_target="tpu_custom_call" | custom-call | tf_op jit(solution)/shard_map/results/pallas_call | solution.py:966
Async XLA Ops:
  1.3 97.8 %copy-start = (bf16[128,1024]{1,0:T(8,128)(2,1)S(1)}, bf16[128,1024]{1,0:T(8,128)(2,1)}, u32[]{:S(2)}) copy-start(bf16[128,1024]{1,0:T(8,128)(2,1)} %tok.1) | copy-start | bytes 786436
  1.3 97.8 %copy-start.1 = (bf16[128,1024]{1,0:T(8,128)(2,1)S(1)}, bf16[128,1024]{1,0:T(8,128)(2,1)}, u32[]{:S(2)}) copy-start(bf16[128,1024]{1,0:T(8,128)(2,1)} %cot.1) | copy-start | bytes 786436

commit v7 on v6

--- a/solution.py
+++ b/solution.py
@@ -850,7 +850,6 @@
     v2 = rcopy(b.vs.at[1], b.vl.at[1], ypeer)
     dtwo = reduce_second(done)
     z_absorb(zgi[0])
-    z_absorb(zgi[1])
     for n in range(STATE):
         parts = [jnp.sum(b.ga[n, e] * b.rate[n, e], axis=0, keepdims=True) for e in range(2)]
         b.sg[LOG_ROW + n : LOG_ROW + n + 1, :] = jnp.concatenate(parts, axis=1) * LN2
@@ -860,6 +859,7 @@
     b.sg[STEP_ROW:LOG_ROW, :] = grad[:RANK]
     for i in range(depth):
         b.sgs[i] = folded(b.sg[:, i * hl : (i + 1) * hl], hl)
+    z_absorb(zgi[1])
     zgs = z_direct(z_scatter(lambda q: b.sgs.at[q], lambda k: b.sgl.at[k], b.sgx))
     v2.wait_recv()
     b.vs[2] = b.vs[1] + b.vl[1]

time: 101 us -> 101 us (level)
  no operation moved by 1% of the time
where the time goes in v7:
time: 101 us
  Pallas kernels  99.6 us (99%)
  between operations  1.34 us (1%)
    pallas_call x1, Pallas kernels, local(): pl.pallas_call(functools.partial(main_kernel, [tuple(group) for group in...  97.8 us

profile of v7, /device:TPU:0, one launch (start us, length us, event | category | flops | bytes accessed | tf_op | source)
XLA Modules:
  0.0 101.0 jit_solution(488594004481733702)
XLA Ops:
  1.3 0.0 copy-start
  1.3 0.0 copy-start.1
  1.3 97.8 %layer.1 = (bf16[128,1024]{1,0:T(8,128)(2,1)S(1)}, bf16[128,1024]{1,0:T(8,128)(2,1)S(1)}, bf16[3,2,64,1024]{3,2,1,0:T(8,128)(2,1)S(1)}, bf16[2,96,128]{2,1,0:T(8,128)(2,1)S(1)}, f32[8,128]{1,0:T(8,128)S(1)}) custom-call(bf16[128,1024]{1,0:T(8,128)(2,1)} %tok.1, bf16[128,1024]{1,0:T(8,128)(2,1)} %cot.1, bf16[1024,128]{1,0:T(8,128)(2,1)} %refs_2_.1, ...), custom_call_target="tpu_custom_call" | custom-call | tf_op jit(solution)/shard_map/layer/pallas_call | solution.py:939
  99.1 0.0 copy-done
  99.1 0.0 copy-done.1
  99.2 1.8 %results.1 = (bf16[128,1024]{1,0:T(8,128)(2,1)}, f32[128,1024]{1,0:T(8,128)}, f32[64]{0:T(128)}, f32[1024,128]{1,0:T(8,128)}, f32[1024,128]{1,0:T(8,128)}, /*ind...) custom-call(bf16[128,1024]{1,0:T(8,128)(2,1)S(1)} %copy-done, ...), custom_call_target="tpu_custom_call" | custom-call | tf_op jit(solution)/shard_map/results/pallas_call | solution.py:966
Async XLA Ops:
  1.3 97.8 %copy-start = (bf16[128,1024]{1,0:T(8,128)(2,1)S(1)}, bf16[128,1024]{1,0:T(8,128)(2,1)}, u32[]{:S(2)}) copy-start(bf16[128,1024]{1,0:T(8,128)(2,1)} %tok.1) | copy-start | bytes 786436
  1.3 97.8 %copy-start.1 = (bf16[128,1024]{1,0:T(8,128)(2,1)S(1)}, bf16[128,1024]{1,0:T(8,128)(2,1)}, u32[]{:S(2)}) copy-start(bf16[128,1024]{1,0:T(8,128)(2,1)} %cot.1) | copy-start | bytes 786436
